TPU v7x, 256 devices: a whole 4x4x8 slice. The times are simulated.
256 devices in a mesh: tm: 16 (over y, x), tile: 16 (over z, core).
Axes of the slice: x: 4, y: 4, z: 8, core: 2. Of those that a mesh axis runs over, the one named last changes fastest.
Arguments:
- latents: bfloat16 [32, 32, 32, 512], P('tm', 'tile'), may hold values from -60 to 60, as said below
- norm_gain: float32 [3, 512], replicated, may hold values from 0.5 to 1.5
- norm_shift: float32 [3, 512], replicated, may hold values from -3 to 3
- conv_weight: bfloat16 [3, 27, 512, 512], P(None, None, 'tile'), may hold values from -0.0546875 to 0.0546875
- conv_bias: float32 [3, 512], P(None, 'tile'), may hold values from -3 to 3
Outputs:
- decoded: bfloat16 [32, 32, 32, 512], P('tm', 'tile')
Inputs may be any that keep to these rules, and one draw needn't show every extreme that they name: Decoder input latents.
All inputs are finite; a program needn't handle non-finite values.
Results may differ from a plain program's by a relative error of at most 0.013.
Values may be sent and summed in bfloat16 or wider, within the bound.
A program may use at most 192 MiB of HBM per device.

v0:
```python
import jax
import jax.numpy as jnp
from jax import lax
from jax.sharding import PartitionSpec as P

C = 512
GROUPS = 32


EPSILON = 1e-06


def prefix(x, axis, combine, identity):
    size, index = (lax.axis_size(axis), lax.axis_index(axis))
    everything = jax.tree.map(lambda part: lax.all_gather(part, axis), x)
    start = jax.tree.map(
        lambda part, zero: jnp.broadcast_to(jnp.asarray(zero, part.dtype), part.shape), x, identity
    )

    def lap(k, before):
        reached = k < index
        new = combine(before, jax.tree.map(lambda part: part[k], everything))
        return jax.tree.map(lambda a, b: jnp.where(reached, a, b), new, before)

    return lax.fori_loop(0, size, lap, start)


def passed_along(value, axis, steps):
    count = lax.axis_size(axis)
    leading, last = (max(0, -steps), min(count, count - steps))
    return lax.ppermute(value, axis, [(source, source + steps) for source in range(leading, last)])


def add_pairs(earlier, later):
    return (earlier[0] + later[0], earlier[1] + later[1])


def causal_prefix(first_sums, second_sums):
    last_first, last_second = (first_sums[-1], second_sums[-1])
    before_first, before_second = prefix(
        (last_first, last_second),
        "tm",
        add_pairs,
        (jnp.zeros_like(last_first), jnp.zeros_like(last_second)),
    )
    return (first_sums + before_first, second_sums + before_second)


def normalize(latent, gain_row, shift_row, frame_cells):
    frames = latent.shape[0]
    group_width = C // GROUPS
    groups_here = latent.shape[3] // group_width
    values = latent.astype(jnp.float32).reshape(frames, -1, groups_here, group_width)
    first_sums = jnp.sum(values, axis=(1, 3))
    second_sums = jnp.sum(values * values, axis=(1, 3))
    first_sums, second_sums = lax.psum((first_sums, second_sums), "tile")
    first_sums, second_sums = causal_prefix(
        jnp.cumsum(first_sums, axis=0), jnp.cumsum(second_sums, axis=0)
    )
    frame_start = lax.axis_index("tm") * frames
    counts = ((frame_start + jnp.arange(frames) + 1) * (frame_cells * group_width)).astype(
        jnp.float32
    )[:, None]
    average = first_sums / counts
    inverse = lax.rsqrt(second_sums / counts - average * average + EPSILON)
    scaled = ((values - average[:, None, :, None]) * inverse[:, None, :, None]).reshape(
        latent.shape
    )
    return jax.nn.silu(scaled * gain_row + shift_row).astype(jnp.bfloat16)


def earlier(active):
    received = passed_along(active, "tm", 1)
    opening = jnp.broadcast_to(active[:1], received.shape)
    received = jnp.where(lax.axis_index("tm") == 0, opening, received)
    return jnp.concatenate([received, active], axis=0)


def apply_kernel(cells, matrix):
    return lax.dot_general(
        cells, matrix, (((1,), (1,)), ((), ())), preferred_element_type=jnp.float32
    )


def convolve(extended, kernel):
    frames = extended.shape[0] - 2
    height, breadth = (extended.shape[1], extended.shape[2])
    spaced = jnp.pad(extended, ((0, 0), (1, 1), (1, 1), (0, 0)))
    summed = jnp.zeros((frames * height * breadth, kernel.shape[1]), jnp.float32)
    for offset in range(27):
        step_t, step_h, step_w = (offset // 9, offset // 3 % 3, offset % 3)
        window_cells = spaced[
            step_t : step_t + frames, step_h : step_h + height, step_w : step_w + breadth, :
        ]
        summed = summed + apply_kernel(
            window_cells.reshape(-1, window_cells.shape[3]), kernel[offset]
        )
    return summed.reshape(frames, height, breadth, kernel.shape[1])


def back_rows(layer, mixed, residual):
    if layer == 1:
        moved = lax.all_to_all(
            mixed.astype(jnp.bfloat16), "tile", split_axis=1, concat_axis=3, tiled=True
        ).astype(mixed.dtype)
        return (residual.astype(jnp.float32) + moved).astype(jnp.bfloat16)
    return lax.all_to_all(
        mixed.astype(jnp.bfloat16), "tile", split_axis=1, concat_axis=3, tiled=True
    )


def on_device(latents, norm_gain, norm_shift, conv_weight, conv_bias):
    frame_cells = latents.shape[1] * lax.axis_size("tile") * latents.shape[2]
    current = latents
    for layer in range(3):
        active = normalize(current, norm_gain[layer], norm_shift[layer], frame_cells)
        whole = lax.all_gather(earlier(active), "tile", axis=1, tiled=True)
        mixed = convolve(whole, conv_weight[layer]) + conv_bias[layer]
        current = back_rows(layer, mixed, latents)
    return current


def solution(mesh):
    placed = (P("tm", "tile", None, None), P(), P(), P(None, None, "tile", None), P(None, "tile"))
    return jax.shard_map(
        on_device,
        mesh=mesh,
        in_specs=placed,
        out_specs=P("tm", "tile", None, None),
        check_vma=False,
    )
```

profile of v0, /device:TPU:3, one launch (start us, length us, event | category | flops | bytes accessed | tf_op | source)
XLA Modules:
  0.0 644.9 jit_solution(8577832631568817750)
XLA Ops:
  9.5 26.6 %all-reduce.5 = (f32[2,32]{1,0:T(2,128)S(1)}, f32[2,32]{1,0:T(2,128)S(1)}) all-reduce(f32[2,32]{1,0:T(2,128)S(1)} %reduce_sum.74, f32[2,32]{1,0:T(2,128)S(1)} %reduce_sum.77), channel_id=1, replica_groups=mesh['tm'=16,'tile'=16] {'tile'}, use_global_device_ids=true, to_apply=%region_2.0 | all-reduce | flops 128 | bytes 1024 | tf_op jit(solution)/shard_map/psum | solution.py:56
  36.1 16.0 %all-gather = f32[16,1,32]{2,1,0:T(1,128)S(1)} all-gather(f32[1,1,32]{2,1,0:T(1,128)S(1)} %slice_bitcast_fusion.11), channel_id=1, replica_groups=mesh['tm'=16,'tile'=16] {'tm'}, dimensions={0}, use_global_device_ids=true | all-gather | bytes 2176 | tf_op jit(solution)/shard_map/all_gather | solution.py:15
  52.1 14.1 %all-gather.1 = f32[16,1,32]{2,1,0:T(1,128)S(1)} all-gather(f32[1,1,32]{2,1,0:T(1,128)S(1)} %slice_bitcast_fusion.10), channel_id=1, replica_groups=mesh['tm'=16,'tile'=16] {'tm'}, dimensions={0}, use_global_device_ids=true | all-gather | bytes 2176 | tf_op jit(solution)/shard_map/all_gather | solution.py:15
  68.3 3.4 collective-permute-start
  71.8 2.3 collective-permute-done
  74.8 52.7 %all-gather.10.cloned.1.call-done = bf16[4,32,32,512]{3,2,1,0:T(8,128)(2,1)} async-done(((bf16[4,2,32,512]{3,2,1,0:T(8,128)(2,1)}), bf16[4,32,32,512]{3,2,1,0:T(8,128)(2,1)}) %all-gather.10.cloned.1.call-update) | async-done | bytes 4194320 | tf_op jit(solution)/shard_map/all_gather | solution.py:117
  127.6 12.6 %pad_slice_fusion.49 = (bf16[2,32,32,512]{3,2,1,0:T(8,128)(2,1)S(1)}, bf16[2,32,32,512]{3,2,1,0:T(8,128)(2,1)}, bf16[2,32,32,512]{3,2,1,0:T(8,128)(2,1)S(1)}, bf...) fusion(bf16[4,32,32,512]{3,2,1,0:T(8,128)(2,1)} %all-gather.10., ...), kind=kLoop, calls=%fused_computation.61 | loop fusion | bytes 27262976 | tf_op jit(solution)/shard_map/slice | solution.py:92
  141.6 20.0 %pad_slice_fusion.48 = (bf16[2,32,32,512]{3,2,1,0:T(8,128)(2,1)}, bf16[2,32,32,512]{3,2,1,0:T(8,128)(2,1)}, bf16[2,32,32,512]{3,2,1,0:T(8,128)(2,1)}, bf16[2,32,...) fusion(bf16[4,32,32,512]{3,2,1,0:T(8,128)(2,1)S(1)} %copy-done), kind=kLoop, calls=%fused_computation.60 | loop fusion | bytes 44040192 | tf_op jit(solution)/shard_map/slice | solution.py:92
  161.7 2.5 convolution_add_fusion.77
  165.8 1.6 convolution_add_fusion.75
  169.1 1.6 convolution_add_fusion.73
  172.4 1.6 convolution_add_fusion.71
  175.7 1.6 convolution_add_fusion.69
  179.0 1.6 convolution_add_fusion.67
  182.2 1.6 convolution_add_fusion.65
  185.5 1.6 convolution_add_fusion.63
  188.8 1.6 convolution_add_fusion.61
  192.1 1.6 convolution_add_fusion.59
  199.9 1.6 convolution_add_fusion.54
  206.5 4.6 all-to-all-start
  211.2 9.1 %all-to-all-done = bf16[16,2,2048]{2,1,0:T(2,128)(2,1)S(1)} async-done(((bf16[16,2,2048]{2,1,0:T(2,128)(2,1)}), bf16[16,2,2048]{2,1,0:T(2,128)(2,1)S(1)}, u32[]{:S(2)}, u32[]{:S(2)}) %all-to-all-start) | async-done | bytes 131104 | tf_op jit(solution)/shard_map/all_to_all | solution.py:107
  223.7 22.9 %all-reduce.4 = (f32[2,32]{1,0:T(2,128)S(1)}, f32[2,32]{1,0:T(2,128)S(1)}) all-reduce(f32[2,32]{1,0:T(2,128)S(1)} %copy.39, f32[2,32]{1,0:T(2,128)S(1)} %copy.40), channel_id=1, replica_groups=mesh['tm'=16,'tile'=16] {'tile'}, use_global_device_ids=true, to_apply=%region_12.13 | all-reduce | flops 128 | bytes 1024 | tf_op jit(solution)/shard_map/psum | solution.py:56
  246.7 15.7 %all-gather.2 = f32[16,1,32]{2,1,0:T(1,128)S(1)} all-gather(f32[1,1,32]{2,1,0:T(1,128)S(1)} %slice_bitcast_fusion.8), channel_id=1, replica_groups=mesh['tm'=16,'tile'=16] {'tm'}, dimensions={0}, use_global_device_ids=true | all-gather | bytes 2176 | tf_op jit(solution)/shard_map/all_gather | solution.py:15
  262.4 14.0 %all-gather.3 = f32[16,1,32]{2,1,0:T(1,128)S(1)} all-gather(f32[1,1,32]{2,1,0:T(1,128)S(1)} %slice_bitcast_fusion.7), channel_id=1, replica_groups=mesh['tm'=16,'tile'=16] {'tm'}, dimensions={0}, use_global_device_ids=true | all-gather | bytes 2176 | tf_op jit(solution)/shard_map/all_gather | solution.py:15
  277.7 2.8 collective-permute-start.1
  280.5 2.9 collective-permute-done.1
  284.1 52.3 %all-gather.12.cloned.1.call-done = bf16[4,32,32,512]{3,2,1,0:T(8,128)(2,1)} async-done(((bf16[4,2,32,512]{3,2,1,0:T(8,128)(2,1)}), bf16[4,32,32,512]{3,2,1,0:T(8,128)(2,1)}) %all-gather.12.cloned.1.call-update) | async-done | bytes 4194320 | tf_op jit(solution)/shard_map/all_gather | solution.py:117
  336.5 12.6 %pad_slice_fusion.25 = (bf16[2,32,32,512]{3,2,1,0:T(8,128)(2,1)S(1)}, bf16[2,32,32,512]{3,2,1,0:T(8,128)(2,1)}, bf16[2,32,32,512]{3,2,1,0:T(8,128)(2,1)S(1)}, bf...) fusion(bf16[4,32,32,512]{3,2,1,0:T(8,128)(2,1)} %all-gather.12., ...), kind=kLoop, calls=%fused_computation.37 | loop fusion | bytes 27262976 | tf_op jit(solution)/shard_map/slice | solution.py:92
  350.5 20.0 %pad_slice_fusion.24 = (bf16[2,32,32,512]{3,2,1,0:T(8,128)(2,1)}, bf16[2,32,32,512]{3,2,1,0:T(8,128)(2,1)}, bf16[2,32,32,512]{3,2,1,0:T(8,128)(2,1)}, bf16[2,32,...) fusion(bf16[4,32,32,512]{3,2,1,0:T(8,128)(2,1)S(1)} %copy-done.1), kind=kLoop, calls=%fused_computation.36 | loop fusion | bytes 44040192 | tf_op jit(solution)/shard_map/slice | solution.py:92
  370.5 2.5 convolution_add_fusion.51
  373.0 1.6 convolution_add_fusion.50
  376.3 1.6 convolution_add_fusion.48
  379.6 1.6 convolution_add_fusion.46
  382.9 1.6 convolution_add_fusion.44
  386.2 1.6 convolution_add_fusion.42
  389.5 1.6 convolution_add_fusion.40
  392.8 1.6 convolution_add_fusion.38
  396.1 1.6 convolution_add_fusion.36
  399.4 1.6 convolution_add_fusion.34
  402.7 1.6 convolution_add_fusion.32
  408.7 1.6 convolution_add_fusion.28
  415.4 4.6 all-to-all-start.1
  420.0 9.1 %all-to-all-done.1 = bf16[16,2,2048]{2,1,0:T(2,128)(2,1)S(1)} async-done(((bf16[16,2,2048]{2,1,0:T(2,128)(2,1)}), bf16[16,2,2048]{2,1,0:T(2,128)(2,1)S(1)}, u32[]{:S(2)}, u32[]{:S(2)}) %all-to-all-start.1) | async-done | bytes 131104 | tf_op jit(solution)/shard_map/all_to_all | solution.py:103
  431.4 22.6 %all-reduce.3 = (f32[2,32]{1,0:T(2,128)S(1)}, f32[2,32]{1,0:T(2,128)S(1)}) all-reduce(f32[2,32]{1,0:T(2,128)S(1)} %reduce_sum.110, f32[2,32]{1,0:T(2,128)S(1)} %reduce_sum.113), channel_id=1, replica_groups=mesh['tm'=16,'tile'=16] {'tile'}, use_global_device_ids=true, to_apply=%region_22.23 | all-reduce | flops 128 | bytes 1024 | tf_op jit(solution)/shard_map/psum | solution.py:56
  454.0 15.7 %all-gather.4 = f32[16,1,32]{2,1,0:T(1,128)S(1)} all-gather(f32[1,1,32]{2,1,0:T(1,128)S(1)} %slice_bitcast_fusion.5), channel_id=1, replica_groups=mesh['tm'=16,'tile'=16] {'tm'}, dimensions={0}, use_global_device_ids=true | all-gather | bytes 2176 | tf_op jit(solution)/shard_map/all_gather | solution.py:15
  469.7 14.0 %all-gather.5 = f32[16,1,32]{2,1,0:T(1,128)S(1)} all-gather(f32[1,1,32]{2,1,0:T(1,128)S(1)} %slice_bitcast_fusion.4), channel_id=1, replica_groups=mesh['tm'=16,'tile'=16] {'tm'}, dimensions={0}, use_global_device_ids=true | all-gather | bytes 2176 | tf_op jit(solution)/shard_map/all_gather | solution.py:15
  485.0 2.8 collective-permute-start.2
  487.8 2.9 collective-permute-done.2
  491.4 52.3 %all-gather.14.cloned.1.call-done = bf16[4,32,32,512]{3,2,1,0:T(8,128)(2,1)} async-done(((bf16[4,2,32,512]{3,2,1,0:T(8,128)(2,1)}), bf16[4,32,32,512]{3,2,1,0:T(8,128)(2,1)}) %all-gather.14.cloned.1.call-update) | async-done | bytes 4194320 | tf_op jit(solution)/shard_map/all_gather | solution.py:117
  543.8 12.8 %pad_slice_fusion.1 = (bf16[2,32,32,512]{3,2,1,0:T(8,128)(2,1)S(1)}, bf16[2,32,32,512]{3,2,1,0:T(8,128)(2,1)}, bf16[2,32,32,512]{3,2,1,0:T(8,128)(2,1)S(1)}, bf1...) fusion(bf16[4,32,32,512]{3,2,1,0:T(8,128)(2,1)} %all-gather.14., ...), kind=kLoop, calls=%fused_computation.13 | loop fusion | bytes 27262976 | tf_op jit(solution)/shard_map/slice | solution.py:92
  558.1 20.0 %pad_slice_fusion = (bf16[2,32,32,512]{3,2,1,0:T(8,128)(2,1)}, bf16[2,32,32,512]{3,2,1,0:T(8,128)(2,1)}, bf16[2,32,32,512]{3,2,1,0:T(8,128)(2,1)}, bf16[2,32,32,...) fusion(bf16[4,32,32,512]{3,2,1,0:T(8,128)(2,1)S(1)} %copy-done.2), kind=kLoop, calls=%fused_computation.12 | loop fusion | bytes 44040192 | tf_op jit(solution)/shard_map/slice | solution.py:92
  578.1 2.4 convolution_add_fusion.25
  580.6 1.6 convolution_add_fusion.24
  582.3 1.6 convolution_add_fusion.23
  585.6 1.6 convolution_add_fusion.21
  588.9 1.6 convolution_add_fusion.19
  592.1 1.6 convolution_add_fusion.17
  595.4 1.6 convolution_add_fusion.15
  598.7 1.6 convolution_add_fusion.13
  602.0 1.6 convolution_add_fusion.11
  605.3 1.6 convolution_add_fusion.9
  608.6 1.6 convolution_add_fusion.7
  616.4 1.6 convolution_add_fusion.2
  622.3 13.5 %all_to_all.36 = bf16[16,2,2048]{2,1,0:T(2,128)(2,1)S(1)} all-to-all(bf16[16,2,2048]{2,1,0:T(2,128)(2,1)S(1)} %reshape.826), channel_id=1, replica_groups=mesh['tm'=16,'tile'=16] {'tile'}, dimensions={0} | all-to-all | bytes 262144 | tf_op jit(solution)/shard_map/all_to_all | solution.py:107
  (332 shorter events, 96.8 us)
Async XLA Ops:
  6.5 68.3 %copy-start.70 = (f32[3,32]{1,0:T(4,128)S(1)}, f32[3,32]{1,0:T(4,128)}, u32[]{:S(2)}) copy-start(f32[3,32]{1,0:T(4,128)} %param.15) | copy-start | bytes 1156
  6.5 121.0 %all-gather.10.cloned.1.call-start = ((), (), s32[]{:S(2)}) async-start(), calls=%async_computation.3 | async-start | bytes 4456448 | tf_op jit(solution)/shard_map/all_gather | solution.py:117
  68.3 5.7 collective-permute-start
  127.6 14.0 %copy-start = (bf16[4,32,32,512]{3,2,1,0:T(8,128)(2,1)S(1)}, bf16[4,32,32,512]{3,2,1,0:T(8,128)(2,1)}, u32[]{:S(2)}) copy-start(bf16[4,32,32,512]{3,2,1,0:T(8,128)(2,1)} %all-gather.10.cloned.1.call-done) | copy-start | bytes 12582916
  161.6 4.1 copy-start.63
  164.1 3.3 copy-start.12
  169.1 3.3 copy-start.54
  170.7 3.3 copy-start.51
  172.4 3.3 copy-start.48
  174.0 3.3 copy-start.45
  175.7 3.3 copy-start.42
  177.3 3.3 copy-start.39
  178.9 3.3 copy-start.9
  180.6 3.3 copy-start.36
  182.2 3.3 copy-start.33
  183.9 3.3 copy-start.30
  185.5 3.3 copy-start.27
  187.2 3.3 copy-start.24
  188.8 3.3 copy-start.21
  190.5 3.3 copy-start.18
  192.1 3.3 copy-start.6
  206.5 13.7 %all-to-all-start = ((bf16[16,2,2048]{2,1,0:T(2,128)(2,1)}), bf16[16,2,2048]{2,1,0:T(2,128)(2,1)S(1)}, u32[]{:S(2)}, u32[]{:S(2)}) async-start(bf16[16,2,2048]{2,1,0:T(2,128)(2,1)} %reshape.822), calls=%async_computation | async-start | bytes 262144 | tf_op jit(solution)/shard_map/all_to_all | solution.py:107
  211.1 125.4 %all-gather.12.cloned.1.call-start = ((), (), s32[]{:S(2)}) async-start(), calls=%async_computation.4 | async-start | bytes 4456448 | tf_op jit(solution)/shard_map/all_gather | solution.py:117
  277.7 5.7 collective-permute-start.1
  336.5 14.0 %copy-start.1 = (bf16[4,32,32,512]{3,2,1,0:T(8,128)(2,1)S(1)}, bf16[4,32,32,512]{3,2,1,0:T(8,128)(2,1)}, u32[]{:S(2)}) copy-start(bf16[4,32,32,512]{3,2,1,0:T(8,128)(2,1)} %all-gather.12.cloned.1.call-done) | copy-start | bytes 12582916
  370.5 4.1 copy-start.64
  373.0 3.3 copy-start.13
  376.3 3.3 copy-start.58
  377.9 3.3 copy-start.55
  379.6 3.3 copy-start.52
  381.2 3.3 copy-start.49
  382.9 3.3 copy-start.46
  384.5 3.3 copy-start.43
  386.2 3.3 copy-start.40
  387.8 3.3 copy-start.10
  389.5 3.3 copy-start.37
  391.1 3.3 copy-start.34
  392.8 3.3 copy-start.31
  394.4 3.3 copy-start.28
  396.1 3.3 copy-start.25
  397.7 3.3 copy-start.22
  399.4 3.3 copy-start.19
  401.0 3.3 copy-start.7
  415.4 13.7 %all-to-all-start.1 = ((bf16[16,2,2048]{2,1,0:T(2,128)(2,1)}), bf16[16,2,2048]{2,1,0:T(2,128)(2,1)S(1)}, u32[]{:S(2)}, u32[]{:S(2)}) async-start(bf16[16,2,2048]{2,1,0:T(2,128)(2,1)} %reshape.824), calls=%async_computation.1 | async-start | bytes 262144 | tf_op jit(solution)/shard_map/all_to_all | solution.py:103
  420.0 123.8 %all-gather.14.cloned.1.call-start = ((), (), s32[]{:S(2)}) async-start(), calls=%async_computation.5 | async-start | bytes 4456448 | tf_op jit(solution)/shard_map/all_gather | solution.py:117
  485.0 5.7 collective-permute-start.2
  543.8 14.3 %copy-start.2 = (bf16[4,32,32,512]{3,2,1,0:T(8,128)(2,1)S(1)}, bf16[4,32,32,512]{3,2,1,0:T(8,128)(2,1)}, u32[]{:S(2)}) copy-start(bf16[4,32,32,512]{3,2,1,0:T(8,128)(2,1)} %all-gather.14.cloned.1.call-done) | copy-start | bytes 12582916
  578.1 4.1 copy-start.65
  580.6 3.3 copy-start.14
  582.3 3.3 copy-start.62
  583.9 3.3 copy-start.59
  585.5 3.3 copy-start.56
  587.2 3.3 copy-start.53
  588.8 3.3 copy-start.50
  590.5 3.3 copy-start.47
  592.1 3.3 copy-start.44
  593.8 3.3 copy-start.41
  595.4 3.3 copy-start.11
  597.1 3.3 copy-start.38
  598.7 3.3 copy-start.35
  600.4 3.3 copy-start.32
  603.7 3.3 copy-start.26
  605.3 3.3 copy-start.23
  608.6 3.3 copy-start.8
  (15 other events, 44.2 us)
Sparse Core Ops, SparseCore 0:
  74.9 52.5 all-gather.9
  284.3 52.1 all-gather.11
  491.6 52.1 all-gather.13
where the time goes:
time: 654 us; the launch traced here: 645 us
  waiting for transfers between devices  184 us (28%)
  blocking collectives  175 us (27%)
  matrix products  131 us (20%)
  local copies, waits for them, and re-layouts  112 us (17%)
  starting transfers between devices  18.3 us (3%)
  between operations  15.1 us (2%)
  other arithmetic  8.84 us (1%)
    all_gather x3, waiting for transfers between devices, on_device(): whole = lax.all_gather(earlier(active), 'tile', axis=1, tiled=True)  157 us
    dot_general x81, matrix products, apply_kernel(): lax.dot_general(cells, matrix, (((1,), (1,)), ((), ())), preferred_elemen...  131 us
    slice x6, local copies, waits for them, and re-layouts, convolve(): spaced[step_t:step_t + frames, step_h:step_h + height, step_w:step_w + br...  98 us
    all_gather x6, blocking collectives, prefix(): everything = jax.tree.map(lambda part: lax.all_gather(part, axis), x)  89.5 us
    psum x3, blocking collectives, normalize(): first_sums, second_sums = lax.psum((first_sums, second_sums), 'tile')  72.1 us
    all_to_all x2, waiting for transfers between devices, back_rows(): lax.all_to_all(mixed.astype(jnp.bfloat16), 'tile', split_axis=1, concat_a...  18.2 us
    all_to_all x1, blocking collectives, back_rows(): lax.all_to_all(mixed.astype(jnp.bfloat16), 'tile', split_axis=1, concat_a...  13.5 us
  transfers between devices with their start and end apart: 8, of which 8 were waited for; matrix products, arithmetic and copies ran while one was open for 0% of the time, Pallas kernels for 0%

commit v1 on v0

v1 whole, which is shorter than its diff:
```python
import jax
import jax.numpy as jnp
from jax import lax
from jax.experimental import pallas as pl
from jax.experimental.pallas import tpu as pltpu
from jax.sharding import PartitionSpec as P

MESH = pl.DeviceIdType.MESH
BF, F32 = jnp.bfloat16, jnp.float32
EPSILON = 1e-06
LAYERS = 3
MAIN = 10 * 256
TOP = MAIN
BOT = MAIN + 512
LANES = MAIN + 1024
HALF = LANES // 2
PER_FRAME = 32 * 32 * 16


def lane_of(shape):
    return lax.broadcasted_iota(jnp.int32, shape, len(shape) - 1)


def roll(x, shift):
    size = x.shape[-1]
    shift = shift % size
    return x if shift == 0 else pltpu.roll(x, shift, axis=x.ndim - 1)


def silu(v):
    return v / (1.0 + jnp.exp(-v))


def kernel(
    lat_ref, gain_ref, shift_ref, w_hbm, bias_ref, out_ref,
    w_ref, local_t, slots_in, raw, top_out, bot_out, top_in, bot_in, top_prev, bot_prev,
    stat_out, stat_in, y_ref, slots_out, final_t, par_ref,
    w_sem, a2a_send, a2a_recv, fin_send, fin_recv, stat_send, stat_recv,
    halo_send, halo_recv, ring_send, ring_recv, sib_send, sib_recv,
):
    tm = lax.axis_index("tm")
    tile = lax.axis_index("tile")
    x, y = lax.rem(tm, 4), lax.div(tm, 4)
    z, core = lax.div(tile, 2), lax.rem(tile, 2)
    chans = pl.multiple_of(tile * 32, 32)
    sibling = z * 2 + (1 - core)
    right = lax.rem(z + 1, 8) * 2 + core
    left = lax.rem(z + 7, 8) * 2 + core

    def remote(src, dst, send, recv, to_tm, to_tile):
        return pltpu.make_async_remote_copy(
            src_ref=src, dst_ref=dst, send_sem=send, recv_sem=recv,
            device_id=(to_tm, to_tile), device_id_type=MESH,
        )

    load_w = pltpu.make_async_copy(w_hbm, w_ref, w_sem)
    load_w.start()

    mine = lat_ref[...].reshape(128, 512).astype(F32)
    local_t[...] = mine.T.astype(BF)
    my_slot = x * 4 + lax.rem(tile, 4)

    def in_copy(t):
        return remote(
            local_t.at[pl.ds(pl.multiple_of(t * 32, 32), 32)], slots_in.at[my_slot],
            a2a_send, a2a_recv, y * 4 + lax.div(tile, 4), t,
        )

    own_x = lax.div(tile, 4) == x

    def send_in(t, carry):
        to_self = jnp.logical_and(t == tile, own_x)

        @pl.when(to_self)
        def _():
            pltpu.make_async_copy(
                local_t.at[pl.ds(pl.multiple_of(t * 32, 32), 32)], slots_in.at[my_slot], a2a_recv
            ).start()

        @pl.when(jnp.logical_not(to_self))
        def _():
            in_copy(t).start()

        return carry

    lax.fori_loop(0, 16, send_in, 0)

    par_ref[...] = jnp.zeros_like(par_ref)
    par_ref[0:3, :] = gain_ref[...]
    par_ref[3:6, :] = shift_ref[...]
    picked = pltpu.roll(par_ref[...], lax.rem(512 - tile * 32, 512), axis=1)[:, :128]
    par_ref[...] = jnp.zeros_like(par_ref)
    par_ref[0:3, 0:32] = bias_ref[...]
    columns = jnp.concatenate([picked, par_ref[:, 0:128], jnp.zeros((112, 128), F32)], axis=0)
    columns = columns.T[0:32]
    par_ref[0:8, 0:128] = columns[0:8]
    par_ref[0:8, 128:256] = columns[8:16]
    par_ref[0:8, 256:384] = columns[16:24]
    par_ref[0:8, 384:512] = columns[24:32]

    def column(index):
        all_columns = jnp.concatenate([par_ref[0:8, 128 * i:128 * i + 128] for i in range(4)], axis=0)
        chosen = jnp.where(lane_of((32, 128)) == index, all_columns, 0.0)
        return jnp.sum(chosen, axis=1, keepdims=True)

    pltpu.make_async_copy(slots_in, slots_in, a2a_recv).wait()
    lane128 = lane_of((32, 128))
    for part in range(4):
        for block in range(2):
            one = slots_in[part * 4 + 2 * block].astype(F32)
            two = slots_in[part * 4 + 2 * block + 1].astype(F32)
            for inner in range(2):
                if inner == 0:
                    frame = jnp.where(lane128 < 64, one, roll(two, 64))
                else:
                    frame = jnp.where(lane128 < 64, roll(one, 64), two)
                at = 256 * (2 + 2 * part + inner) + 128 * block
                raw[0, :, at:at + 128] = frame.astype(BF)

    lane256 = lane_of((32, 256))
    col256, row256 = lax.rem(lane256, 32), lax.div(lane256, 32)

    def ring_copy(layer, way, step):
        back = (step - 1) if way == 0 else (1 - step)
        owner = lax.rem(z - back + 8, 8) * 2 + core
        rows = pl.ds(pl.multiple_of(owner * 32, 32), 32)
        lanes = slice(0, LANES)
        if step == 4:
            lanes = slice(0, HALF) if way == 0 else slice(HALF, LANES)
        piece = y_ref.at[layer, rows, lanes]
        return remote(
            piece, piece, ring_send.at[layer, way * 4 + step - 1], ring_recv.at[layer, way * 4 + step - 1],
            tm, right if way == 0 else left,
        )

    def sib_copy(layer, back, lanes, index):
        owner = lax.rem(z - back + 8, 8) * 2 + core
        rows = pl.ds(pl.multiple_of(owner * 32, 32), 32)
        piece = y_ref.at[layer, rows, lanes]
        return remote(piece, piece, sib_send.at[layer, index], sib_recv.at[layer, index], tm, sibling)

    whole = slice(0, LANES)
    sib_parts = [
        (0, whole, 0), (1, whole, 1), (-1, whole, 2), (2, whole, 3), (-2, whole, 4),
        (3, whole, 5), (-3, whole, 6), (4, slice(0, HALF), 7), (-4, slice(HALF, LANES), 8),
    ]

    def halo_copies(layer):
        to_left, to_right = lax.rem(x + 3, 4), lax.rem(x + 1, 4)
        later = lax.rem(y + 1, 4)
        plan = [
            (top_out, bot_in, y * 4 + to_left), (bot_out, top_in, y * 4 + to_right),
            (top_out, bot_prev, later * 4 + to_left), (bot_out, top_prev, later * 4 + to_right),
        ]
        copies = [
            remote(src.at[layer], dst.at[layer], halo_send.at[layer, i], halo_recv.at[layer, i], to, tile)
            for i, (src, dst, to) in enumerate(plan)
        ]
        copies.append(remote(
            raw.at[layer, :, 256 * 8:256 * 10], raw.at[layer, :, 0:512],
            halo_send.at[layer, 4], halo_recv.at[layer, 4], later * 4 + x, tile,
        ))
        return copies

    def stat_copy(layer, k):
        other = lax.rem(tm + k, 16)
        return remote(
            stat_out.at[layer], stat_in.at[layer, 15 - k], stat_send.at[layer], stat_recv.at[layer], other, tile
        )

    def layer_step(layer, carry):
        halos = halo_copies(layer)
        halos[4].start()
        sums = jnp.zeros((32, 128), F32)
        tops = [jnp.zeros((32, 128), F32)] * 2
        bots = [jnp.zeros((32, 128), F32)] * 2
        for f in range(8):
            values = raw[layer, :, 256 * (f + 2):256 * (f + 3)].astype(F32)
            first = jnp.sum(values, axis=1, keepdims=True)
            second = jnp.sum(values * values, axis=1, keepdims=True)
            sums = jnp.where(lane128 == f, first, sums)
            sums = jnp.where(lane128 == 8 + f, second, sums)
            slot = f // 2
            here = lax.div(lane128, 32) == slot
            tops[f % 2] = jnp.where(here, roll(values[:, :128], 32 * slot), tops[f % 2])
            bots[f % 2] = jnp.where(here, roll(values[:, 128:], 32 * slot - 96), bots[f % 2])
        for i in range(2):
            top_out[layer, :, 128 * i:128 * i + 128] = tops[i].astype(BF)
            bot_out[layer, :, 128 * i:128 * i + 128] = bots[i].astype(BF)
        low = jnp.sum(sums[0:16], axis=0, keepdims=True)
        high = jnp.sum(sums[16:32], axis=0, keepdims=True)
        sub8 = lax.broadcasted_iota(jnp.int32, (8, 128), 0)
        stat_out[layer] = jnp.where(sub8 == 0, low, jnp.where(sub8 == 1, high, 0.0))

        def send_stat(k, c):
            stat_copy(layer, k).start()
            return c

        lax.fori_loop(1, 16, send_stat, 0)
        for copy in halos[:4]:
            copy.start()

        pltpu.make_async_copy(stat_in.at[layer], stat_in.at[layer], stat_recv.at[layer]).wait()
        mask_lane = lax.broadcasted_iota(jnp.int32, (128, 128), 0)
        mask_col = lax.broadcasted_iota(jnp.int32, (128, 128), 1)
        wanted = jnp.maximum(8 * y - 2 + lax.rem(mask_col, 16), 0)
        fits = (mask_lane < 16) & (mask_col < 32) & (lax.div(mask_lane, 8) == lax.div(mask_col, 16))
        sources = [jnp.zeros((8, 128), F32)] * 4
        for s in range(16):
            block = stat_out[layer] if s == 15 else stat_in[layer, s]
            from_y = lax.div(lax.rem(tm + 16 - (15 - s), 16), 4)
            for q in range(4):
                sources[q] = sources[q] + jnp.where(from_y == q, block, 0.0)
        cumulative = jnp.zeros((8, 128), F32)
        for q in range(4):
            mask = jnp.where(fits & (8 * q + lax.rem(mask_lane, 8) <= wanted), 1.0, 0.0)
            cumulative = cumulative + lax.dot_general(
                sources[q], mask, (((1,), (0,)), ((), ())),
                precision=lax.Precision.HIGHEST, preferred_element_type=F32,
            )
        lane8 = lane_of((8, 128))
        count = ((jnp.maximum(8 * y - 2 + lax.rem(lane8, 16), 0) + 1) * PER_FRAME).astype(F32)
        average = cumulative / count
        spread = roll(average, -16)
        inverse = lax.rsqrt(spread - average * average + EPSILON)
        low_half = lax.broadcasted_iota(jnp.int32, (32, 128), 0) < 16
        average = jnp.where(low_half, average[0:1], average[1:2])
        inverse = jnp.where(low_half, inverse[0:1], inverse[1:2])
        gain, shift = column(layer), column(3 + layer)

        def normal(values, mean_at, inverse_at):
            return silu(((values - mean_at) * inverse_at) * gain + shift)

        for copy in halos:
            copy.wait_recv()
        mine = pl.ds(chans, 32)
        opening = y == 0
        for j in range(10):
            values = raw[layer, :, 256 * j:256 * j + 256].astype(F32)
            if j < 2:
                values = jnp.where(opening, raw[layer, :, 512:768].astype(F32), values)
            done = normal(values, average[:, j:j + 1], inverse[:, j:j + 1])
            y_ref[layer, mine, 256 * j:256 * j + 256] = done.astype(BF)
        slot128 = lax.div(lane128, 32)
        for base, now, before, outside in (
            (TOP, top_in, top_prev, x == 0), (BOT, bot_in, bot_prev, x == 3),
        ):
            even = now[layer, :, 0:128].astype(F32)
            for b in range(4):
                own = now[layer, :, 128 * (b % 2):128 * (b % 2) + 128].astype(F32)
                values = own
                if b < 2:
                    earlier = roll(before[layer, :, 128 * b:128 * b + 128].astype(F32), 32)
                    earlier = jnp.where(opening, even, earlier)
                    values = jnp.where(slot128 == 0, earlier, roll(own, 32))
                mean_at, inverse_at = average[:, b:b + 1], inverse[:, b:b + 1]
                for s in range(1, 4):
                    j = b + 2 * s
                    mean_at = jnp.where(slot128 == s, average[:, j:j + 1], mean_at)
                    inverse_at = jnp.where(slot128 == s, inverse[:, j:j + 1], inverse_at)
                done = jnp.where(outside, 0.0, normal(values, mean_at, inverse_at))
                y_ref[layer, mine, base + 128 * b:base + 128 * b + 128] = done.astype(BF)

        ring_copy(layer, 0, 1).start()
        ring_copy(layer, 1, 1).start()
        sib_copy(layer, *sib_parts[0]).start()
        for step in range(1, 5):
            for way in (0, 1):
                ring_copy(layer, way, step).wait_recv()
                if step < 4:
                    ring_copy(layer, way, step + 1).start()
                sib_copy(layer, *sib_parts[2 * step - 1 + way]).start()
        for part in sib_parts:
            sib_copy(layer, *part).wait_recv()

        @pl.when(layer == 0)
        def _():
            load_w.wait()

        def product(first_offset, count, lanes_at):
            total = None
            for dt in range(3):
                matrix = w_ref[layer, pl.ds(9 * dt + first_offset, count)].reshape(32 * count, 512)
                cells = y_ref[layer, :, lanes_at(dt)]
                term = lax.dot_general(
                    matrix, cells, (((1,), (0,)), ((), ())), preferred_element_type=F32
                )
                total = term if total is None else total + term
            return total

        def across(total):
            before = jnp.where(col256 >= 1, roll(total[0:32], 1), 0.0)
            after = jnp.where(col256 <= 30, roll(total[64:96], -1), 0.0)
            return before + total[32:64] + after

        upper = across(product(0, 3, lambda dt: slice(TOP + 128 * dt, TOP + 128 * dt + 256)))
        lower = across(product(6, 3, lambda dt: slice(BOT + 128 * dt, BOT + 128 * dt + 256)))
        bias = column(8 + layer)
        keep = jnp.where(layer == 1, 1.0, 0.0)
        for f in range(8):
            total = product(0, 9, lambda dt: slice(256 * (f + dt), 256 * (f + dt) + 256))
            above = roll(across(total[0:96]), 32)
            below = roll(across(total[192:288]), -32)
            slot = f // 2
            edge = 128 * (f % 2)
            from_upper = roll(upper[:, edge:edge + 128], -32 * slot)
            from_lower = roll(lower[:, edge:edge + 128], 96 - 32 * slot)
            zero = jnp.zeros((32, 128), F32)
            above = jnp.where(row256 == 0, jnp.concatenate([from_upper, zero], axis=1), above)
            below = jnp.where(row256 == 7, jnp.concatenate([zero, from_lower], axis=1), below)
            result = above + across(total[96:192]) + below + bias
            result = result + keep * raw[0, :, 256 * (f + 2):256 * (f + 3)].astype(F32)
            raw[layer + 1, :, 256 * (f + 2):256 * (f + 3)] = result.astype(BF)
        return carry

    lax.fori_loop(0, LAYERS, layer_step, 0)

    for part in range(4):
        for block in range(2):
            at = 256 * (2 + 2 * part) + 128 * block
            one = raw[LAYERS, :, at:at + 128].astype(F32)
            two = raw[LAYERS, :, at + 256:at + 384].astype(F32)
            slots_out[part * 4 + 2 * block] = jnp.where(lane128 < 64, one, roll(two, 64)).astype(BF)
            slots_out[part * 4 + 2 * block + 1] = jnp.where(lane128 < 64, roll(one, 64), two).astype(BF)

    def send_out(slot, c):
        to_tm = y * 4 + lax.div(slot, 4)
        to_tile = x * 4 + lax.rem(slot, 4)
        to_self = jnp.logical_and(to_tm == tm, to_tile == tile)
        rows = final_t.at[pl.ds(chans, 32)]

        @pl.when(to_self)
        def _():
            pltpu.make_async_copy(slots_out.at[slot], rows, fin_recv).start()

        @pl.when(jnp.logical_not(to_self))
        def _():
            remote(slots_out.at[slot], rows, fin_send, fin_recv, to_tm, to_tile).start()

        return c

    lax.fori_loop(0, 16, send_out, 0)
    pltpu.make_async_copy(final_t, final_t, fin_recv).wait()
    out_ref[...] = final_t[...].astype(F32).T.astype(BF).reshape(2, 2, 32, 512)


    def sent(ref, sem):
        @pl.when(own_x)
        def _():
            pltpu.make_async_copy(ref.at[0:15], ref.at[0:15], sem).wait()

        @pl.when(jnp.logical_not(own_x))
        def _():
            pltpu.make_async_copy(ref, ref, sem).wait()

    sent(slots_in, a2a_send)
    sent(slots_out, fin_send)

    def drain(layer, c):
        for copy in halo_copies(layer):
            copy.wait_send()
        pltpu.make_async_copy(stat_in.at[layer], stat_in.at[layer], stat_send.at[layer]).wait()
        for step in range(1, 5):
            for way in (0, 1):
                ring_copy(layer, way, step).wait_send()
        for part in sib_parts:
            sib_copy(layer, *part).wait_send()
        return c

    lax.fori_loop(0, LAYERS, drain, 0)


def on_device(latents, norm_gain, norm_shift, conv_weight, conv_bias):
    vmem = pl.BlockSpec(memory_space=pltpu.VMEM)
    dma = pltpu.SemaphoreType.DMA
    return pl.pallas_call(
        kernel,
        out_shape=jax.ShapeDtypeStruct((2, 2, 32, 512), BF),
        in_specs=[vmem, vmem, vmem, pl.BlockSpec(memory_space=pl.ANY), vmem],
        out_specs=vmem,
        scratch_shapes=[
            pltpu.VMEM((3, 27, 32, 512), BF),
            pltpu.VMEM((512, 128), BF),
            pltpu.VMEM((16, 32, 128), BF),
            pltpu.VMEM((4, 32, MAIN), BF),
            pltpu.VMEM((3, 32, 256), BF),
            pltpu.VMEM((3, 32, 256), BF),
            pltpu.VMEM((3, 32, 256), BF),
            pltpu.VMEM((3, 32, 256), BF),
            pltpu.VMEM((3, 32, 256), BF),
            pltpu.VMEM((3, 32, 256), BF),
            pltpu.VMEM((3, 8, 128), F32),
            pltpu.VMEM((3, 15, 8, 128), F32),
            pltpu.VMEM((3, 512, LANES), BF),
            pltpu.VMEM((16, 32, 128), BF),
            pltpu.VMEM((512, 128), BF),
            pltpu.VMEM((8, 512), F32),
            dma, dma, dma, dma, dma, dma((3,)), dma((3,)),
            dma((3, 5)), dma((3, 5)), dma((3, 8)), dma((3, 8)), dma((3, 9)), dma((3, 9)),
        ],
        compiler_params=pltpu.CompilerParams(
            has_side_effects=True, vmem_limit_bytes=50 * 1024 * 1024
        ),
        cost_estimate=pl.CostEstimate(flops=8 * 10**9, bytes_accessed=3 * 10**6, transcendentals=10**6),
    )(latents, norm_gain, norm_shift, conv_weight, conv_bias)


def solution(mesh):
    placed = (P("tm", "tile", None, None), P(), P(), P(None, None, "tile", None), P(None, "tile"))
    return jax.shard_map(
        on_device,
        mesh=mesh,
        in_specs=placed,
        out_specs=P("tm", "tile", None, None),
        check_vma=False,
    )
```

time: 654 us -> 142 us (0.22); the launches traced: 645 us -> 141 us
  waiting for transfers between devices: 184 us -> 0 us
  blocking collectives: 175 us -> 0 us
  Pallas kernels: 0 us -> 135 us
  matrix products: 131 us -> 0 us
  local copies, waits for them, and re-layouts: 112 us -> 5.38 us
  starting transfers between devices: 18.3 us -> 0 us
  between operations: 15.1 us -> 0.01 us
  other arithmetic: 8.84 us -> 0 us
    all_gather x3 -> x0, waiting for transfers between devices: 157 us -> none  [on_device(): whole = lax.all_gather(earlier(active), 'tile', axis=1, tiled=True)]
    pallas_call x0 -> x1, Pallas kernels: none -> 135 us  [on_device(): pl.pallas_call(kernel, out_shape=jax.ShapeDtypeStruct((2, 2, 32, 512), BF...]
    dot_general x81 -> x0, matrix products: 131 us -> none  [apply_kernel(): lax.dot_general(cells, matrix, (((1,), (1,)), ((), ())), preferred_elemen...]
    slice x8 -> x0, local copies, waits for them, and re-layouts: 99.6 us -> none  [the longest x6 98 us: convolve(): spaced[step_t:step_t + frames, step_h:step_h + height, step_w:step_w + br...]
    all_gather x6 -> x0, blocking collectives: 89.5 us -> none  [prefix(): everything = jax.tree.map(lambda part: lax.all_gather(part, axis), x)]
    psum x3 -> x0, blocking collectives: 72.1 us -> none  [normalize(): first_sums, second_sums = lax.psum((first_sums, second_sums), 'tile')]
    all_to_all x2 -> x0, waiting for transfers between devices: 18.2 us -> none  [back_rows(): lax.all_to_all(mixed.astype(jnp.bfloat16), 'tile', split_axis=1, concat_a...]
    all_to_all x1 -> x0, blocking collectives: 13.5 us -> none  [back_rows(): lax.all_to_all(mixed.astype(jnp.bfloat16), 'tile', split_axis=1, concat_a...]
  transfers between devices with their start and end apart: 8 -> 0, of which waited for: 8 -> 0; matrix products, arithmetic and copies ran while one was open for 0% -> 0% of each run, Pallas kernels for 0% -> 0%
where the time goes in v1:
time: 142 us; the launch traced here: 141 us
  Pallas kernels  135 us (95%)
  local copies, waits for them, and re-layouts  5.38 us (4%)
    pallas_call x1, Pallas kernels, on_device(): pl.pallas_call(kernel, out_shape=jax.ShapeDtypeStruct((2, 2, 32, 512), BF...  135 us
    unnamed x11, local copies, waits for them, and re-layouts  5.38 us

profile of v1, /device:TPU:3, one launch (start us, length us, event | category | flops | bytes accessed | tf_op | source)
XLA Modules:
  0.0 140.8 jit_solution(10308965582522697743)
XLA Ops:
  0.0 0.0 copy-start
  0.0 1.7 %copy-done = bf16[3,27,32,512]{3,2,1,0:T(8,128)(2,1)S(1)} copy-done((bf16[3,27,32,512]{3,2,1,0:T(8,128)(2,1)S(1)}, bf16[3,27,32,512]{3,2,1,0:T(8,128)(2,1)}, u32[]{:S(2)}) %copy-start) | copy-done | bytes 2654232
  1.8 0.0 copy-start.1
  1.8 0.9 copy-done.1
  2.7 0.0 copy-start.2
  2.7 0.7 copy-done.2
  3.4 0.0 copy-start.3
  3.4 0.7 copy-done.3
  4.0 0.0 copy-start.4
  4.1 0.7 copy-done.4
  4.7 135.4 %shard_map.55 = bf16[2,2,32,512]{3,2,1,0:T(8,128)(2,1)S(1)} custom-call(bf16[2,2,32,512]{3,2,1,0:T(8,128)(2,1)S(1)} %copy-done.1, f32[3,512]{1,0:T(4,128)S(1)} %copy-done.2, f32[3,512]{1,0:T(4,128)S(1)} %copy-done.3, bf16[3,27,32,512]{3,2,1,0:T(8,128)(2,1)S(1)} %copy-done, f32[3,32]{1,0:T(4,128)S(1)} %copy-done.4), custom_call_target="tpu_custom_call" | custom-call | flops 8000000000 | bytes 3000000 | tf_op jit(solution)/shard_map/pallas_call | solution.py:376
  140.2 0.7 copy.7
Async XLA Ops:
  0.0 1.7 %copy-start = (bf16[3,27,32,512]{3,2,1,0:T(8,128)(2,1)S(1)}, bf16[3,27,32,512]{3,2,1,0:T(8,128)(2,1)}, u32[]{:S(2)}) copy-start(bf16[3,27,32,512]{3,2,1,0:T(8,128)(2,1)} %w_hbm.1) | copy-start | bytes 7962628
  1.8 0.9 copy-start.1
  2.7 0.7 copy-start.2
  3.4 0.7 copy-start.3
  4.0 0.7 copy-start.4

commit v2 on v1

--- a/solution.py
+++ b/solution.py
@@ -11,9 +11,11 @@
 LAYERS = 3
 MAIN = 10 * 256
 TOP = MAIN
-BOT = MAIN + 512
-LANES = MAIN + 1024
-HALF = LANES // 2
+BOT = MAIN + 256
+PREV = MAIN + 512
+LANES = MAIN + 640
+CHUNKS = ((0, 1664), (1664, LANES))
+PARTS = len(CHUNKS)
 PER_FRAME = 32 * 32 * 16
 
 
@@ -32,10 +34,11 @@
 
 
 def kernel(
-    lat_ref, gain_ref, shift_ref, w_hbm, bias_ref, out_ref,
+    lat_hbm, gain_hbm, shift_hbm, w_hbm, bias_hbm, out_ref,
+    lat_ref, gain_ref, shift_ref, bias_ref,
     w_ref, local_t, slots_in, raw, top_out, bot_out, top_in, bot_in, top_prev, bot_prev,
     stat_out, stat_in, y_ref, slots_out, final_t, par_ref,
-    w_sem, a2a_send, a2a_recv, fin_send, fin_recv, stat_send, stat_recv,
+    in_sem, w_sem, a2a_send, a2a_recv, fin_send, fin_recv, stat_send, stat_recv,
     halo_send, halo_recv, ring_send, ring_recv, sib_send, sib_recv,
 ):
     tm = lax.axis_index("tm")
@@ -54,8 +57,48 @@
         )
 
     load_w = pltpu.make_async_copy(w_hbm, w_ref, w_sem)
+    loads = [
+        pltpu.make_async_copy(src, dst, in_sem.at[i])
+        for i, (src, dst) in enumerate((
+            (lat_hbm, lat_ref), (gain_hbm, gain_ref), (shift_hbm, shift_ref), (bias_hbm, bias_ref),
+        ))
+    ]
+    for load in loads:
+        load.start()
     load_w.start()
 
+    barrier = pltpu.get_barrier_semaphore()
+    own_x = lax.div(tile, 4) == x
+
+    def greet(to_tm, to_tile):
+        pl.semaphore_signal(barrier, inc=1, device_id=(to_tm, to_tile), device_id_type=MESH)
+
+    def greet_tm(k, c):
+        greet(lax.rem(tm + k, 16), tile)
+        return c
+
+    def greet_a2a(k, c):
+        to_tm = y * 4 + lax.div(tile, 4)
+
+        @pl.when(jnp.logical_not(jnp.logical_and(to_tm == tm, k == tile)))
+        def _():
+            greet(to_tm, k)
+
+        from_tm, from_tile = y * 4 + lax.div(k, 4), x * 4 + lax.rem(k, 4)
+
+        @pl.when(jnp.logical_not(jnp.logical_and(from_tm == tm, from_tile == tile)))
+        def _():
+            greet(from_tm, from_tile)
+
+        return c
+
+    lax.fori_loop(0, 16, greet_a2a, 0)
+    lax.fori_loop(1, 16, greet_tm, 0)
+    greet(tm, sibling)
+    greet(tm, left)
+    greet(tm, right)
+
+    loads[0].wait()
     mine = lat_ref[...].reshape(128, 512).astype(F32)
     local_t[...] = mine.T.astype(BF)
     my_slot = x * 4 + lax.rem(tile, 4)
@@ -66,8 +109,6 @@
             a2a_send, a2a_recv, y * 4 + lax.div(tile, 4), t,
         )
 
-    own_x = lax.div(tile, 4) == x
-
     def send_in(t, carry):
         to_self = jnp.logical_and(t == tile, own_x)
 
@@ -83,8 +124,11 @@
 
         return carry
 
+    pl.semaphore_wait(barrier, jnp.where(own_x, 48, 50))
     lax.fori_loop(0, 16, send_in, 0)
 
+    for load in loads[1:]:
+        load.wait()
     par_ref[...] = jnp.zeros_like(par_ref)
     par_ref[0:3, :] = gain_ref[...]
     par_ref[3:6, :] = shift_ref[...]
@@ -120,29 +164,30 @@
     lane256 = lane_of((32, 256))
     col256, row256 = lax.rem(lane256, 32), lax.div(lane256, 32)
 
-    def ring_copy(layer, way, step):
+    def ring_copy(layer, way, step, part):
         back = (step - 1) if way == 0 else (1 - step)
         owner = lax.rem(z - back + 8, 8) * 2 + core
         rows = pl.ds(pl.multiple_of(owner * 32, 32), 32)
-        lanes = slice(0, LANES)
-        if step == 4:
-            lanes = slice(0, HALF) if way == 0 else slice(HALF, LANES)
-        piece = y_ref.at[layer, rows, lanes]
+        piece = y_ref.at[layer, rows, slice(*CHUNKS[part])]
+        at = (way * 4 + step - 1) * PARTS + part
         return remote(
-            piece, piece, ring_send.at[layer, way * 4 + step - 1], ring_recv.at[layer, way * 4 + step - 1],
-            tm, right if way == 0 else left,
+            piece, piece, ring_send.at[layer, at], ring_recv.at[layer, at], tm, right if way == 0 else left
         )
 
-    def sib_copy(layer, back, lanes, index):
+    ring_order = [
+        (way, step, part)
+        for step in range(1, 5) for part in range(PARTS) for way in (0, 1)
+        if step < 4 or (part < PARTS // 2) == (way == 0)
+    ]
+
+    def sib_copy(layer, back, lanes, at):
         owner = lax.rem(z - back + 8, 8) * 2 + core
         rows = pl.ds(pl.multiple_of(owner * 32, 32), 32)
-        piece = y_ref.at[layer, rows, lanes]
-        return remote(piece, piece, sib_send.at[layer, index], sib_recv.at[layer, index], tm, sibling)
-
-    whole = slice(0, LANES)
-    sib_parts = [
-        (0, whole, 0), (1, whole, 1), (-1, whole, 2), (2, whole, 3), (-2, whole, 4),
-        (3, whole, 5), (-3, whole, 6), (4, slice(0, HALF), 7), (-4, slice(HALF, LANES), 8),
+        piece = y_ref.at[layer, rows, slice(*lanes)]
+        return remote(piece, piece, sib_send.at[layer, at], sib_recv.at[layer, at], tm, sibling)
+
+    sib_order = [(0, (0, LANES), 0)] + [
+        (step if way == 0 else -step, CHUNKS[part], 1 + i) for i, (way, step, part) in enumerate(ring_order)
     ]
 
     def halo_copies(layer):
@@ -242,36 +287,42 @@
             done = normal(values, average[:, j:j + 1], inverse[:, j:j + 1])
             y_ref[layer, mine, 256 * j:256 * j + 256] = done.astype(BF)
         slot128 = lax.div(lane128, 32)
-        for base, now, before, outside in (
-            (TOP, top_in, top_prev, x == 0), (BOT, bot_in, bot_prev, x == 3),
-        ):
-            even = now[layer, :, 0:128].astype(F32)
-            for b in range(4):
-                own = now[layer, :, 128 * (b % 2):128 * (b % 2) + 128].astype(F32)
-                values = own
-                if b < 2:
-                    earlier = roll(before[layer, :, 128 * b:128 * b + 128].astype(F32), 32)
-                    earlier = jnp.where(opening, even, earlier)
-                    values = jnp.where(slot128 == 0, earlier, roll(own, 32))
-                mean_at, inverse_at = average[:, b:b + 1], inverse[:, b:b + 1]
+        for base, now, outside in ((TOP, top_in, x == 0), (BOT, bot_in, x == 3)):
+            for b in range(2):
+                values = now[layer, :, 128 * b:128 * b + 128].astype(F32)
+                mean_at, inverse_at = average[:, b + 2:b + 3], inverse[:, b + 2:b + 3]
                 for s in range(1, 4):
-                    j = b + 2 * s
+                    j = b + 2 + 2 * s
                     mean_at = jnp.where(slot128 == s, average[:, j:j + 1], mean_at)
                     inverse_at = jnp.where(slot128 == s, inverse[:, j:j + 1], inverse_at)
                 done = jnp.where(outside, 0.0, normal(values, mean_at, inverse_at))
                 y_ref[layer, mine, base + 128 * b:base + 128 * b + 128] = done.astype(BF)
-
-        ring_copy(layer, 0, 1).start()
-        ring_copy(layer, 1, 1).start()
-        sib_copy(layer, *sib_parts[0]).start()
-        for step in range(1, 5):
+        values = jnp.zeros((32, 128), F32)
+        for i, (now, before) in enumerate(((top_in, top_prev), (bot_in, bot_prev))):
+            first = now[layer, :, 0:128].astype(F32)
+            for b in range(2):
+                last = before[layer, :, 128 * b:128 * b + 128].astype(F32)
+                slot = 2 * i + b
+                moved = jnp.where(opening, roll(first, 32 * slot), roll(last, 32 * slot - 96))
+                values = jnp.where(slot128 == slot, moved, values)
+        odd = lax.rem(slot128, 2) == 1
+        mean_at = jnp.where(odd, average[:, 1:2], average[:, 0:1])
+        inverse_at = jnp.where(odd, inverse[:, 1:2], inverse[:, 0:1])
+        done = normal(values, mean_at, inverse_at)
+        done = jnp.where((slot128 < 2) & (x == 0) | (slot128 >= 2) & (x == 3), 0.0, done)
+        y_ref[layer, mine, PREV:PREV + 128] = done.astype(BF)
+
+        for part in range(PARTS):
             for way in (0, 1):
-                ring_copy(layer, way, step).wait_recv()
-                if step < 4:
-                    ring_copy(layer, way, step + 1).start()
-                sib_copy(layer, *sib_parts[2 * step - 1 + way]).start()
-        for part in sib_parts:
-            sib_copy(layer, *part).wait_recv()
+                ring_copy(layer, way, 1, part).start()
+        sib_copy(layer, *sib_order[0]).start()
+        for i, (way, step, part) in enumerate(ring_order):
+            ring_copy(layer, way, step, part).wait_recv()
+            if (way, step + 1, part) in ring_order:
+                ring_copy(layer, way, step + 1, part).start()
+            sib_copy(layer, *sib_order[1 + i]).start()
+        for entry in sib_order:
+            sib_copy(layer, *entry).wait_recv()
 
         @pl.when(layer == 0)
         def _():
@@ -293,8 +344,34 @@
             after = jnp.where(col256 <= 30, roll(total[64:96], -1), 0.0)
             return before + total[32:64] + after
 
-        upper = across(product(0, 3, lambda dt: slice(TOP + 128 * dt, TOP + 128 * dt + 256)))
-        lower = across(product(6, 3, lambda dt: slice(BOT + 128 * dt, BOT + 128 * dt + 256)))
+        def edge_rows(base, first_offset, slot):
+            early, late, now = [
+                lax.dot_general(
+                    w_ref[layer, pl.ds(9 * dt + first_offset, 3)].reshape(96, 512),
+                    y_ref[layer, :, base:base + 256],
+                    (((1,), (0,)), ((), ())), preferred_element_type=F32,
+                )
+                for dt in range(3)
+            ]
+            before, middle = [
+                lax.dot_general(
+                    w_ref[layer, pl.ds(9 * dt + first_offset, 3)].reshape(96, 512),
+                    y_ref[layer, :, PREV:PREV + 128],
+                    (((1,), (0,)), ((), ())), preferred_element_type=F32,
+                )
+                for dt in range(2)
+            ]
+            slots = lax.div(lane_of((96, 128)), 32)
+            even = roll(early[:, :128] + late[:, 128:], 32)
+            odd = roll(early[:, 128:], 32)
+            even = jnp.where(slots == 0, roll(before, -32 * slot) + roll(middle, -32 * slot - 32), even)
+            odd = jnp.where(slots == 0, roll(before, -32 * slot - 32), odd)
+            even = even + now[:, :128]
+            odd = odd + late[:, :128] + now[:, 128:]
+            return across(jnp.concatenate([even, odd], axis=1))
+
+        upper = edge_rows(TOP, 0, 0)
+        lower = edge_rows(BOT, 6, 2)
         bias = column(8 + layer)
         keep = jnp.where(layer == 1, 1.0, 0.0)
         for f in range(8):
@@ -360,11 +437,10 @@
         for copy in halo_copies(layer):
             copy.wait_send()
         pltpu.make_async_copy(stat_in.at[layer], stat_in.at[layer], stat_send.at[layer]).wait()
-        for step in range(1, 5):
-            for way in (0, 1):
-                ring_copy(layer, way, step).wait_send()
-        for part in sib_parts:
-            sib_copy(layer, *part).wait_send()
+        for entry in ring_order:
+            ring_copy(layer, *entry).wait_send()
+        for entry in sib_order:
+            sib_copy(layer, *entry).wait_send()
         return c
 
     lax.fori_loop(0, LAYERS, drain, 0)
@@ -376,9 +452,13 @@
     return pl.pallas_call(
         kernel,
         out_shape=jax.ShapeDtypeStruct((2, 2, 32, 512), BF),
-        in_specs=[vmem, vmem, vmem, pl.BlockSpec(memory_space=pl.ANY), vmem],
+        in_specs=[pl.BlockSpec(memory_space=pltpu.HBM)] * 5,
         out_specs=vmem,
         scratch_shapes=[
+            pltpu.VMEM((2, 2, 32, 512), BF),
+            pltpu.VMEM((3, 512), F32),
+            pltpu.VMEM((3, 512), F32),
+            pltpu.VMEM((3, 32), F32),
             pltpu.VMEM((3, 27, 32, 512), BF),
             pltpu.VMEM((512, 128), BF),
             pltpu.VMEM((16, 32, 128), BF),
@@ -395,11 +475,11 @@
             pltpu.VMEM((16, 32, 128), BF),
             pltpu.VMEM((512, 128), BF),
             pltpu.VMEM((8, 512), F32),
-            dma, dma, dma, dma, dma, dma((3,)), dma((3,)),
-            dma((3, 5)), dma((3, 5)), dma((3, 8)), dma((3, 8)), dma((3, 9)), dma((3, 9)),
+            dma((4,)), dma, dma, dma, dma, dma, dma((3,)), dma((3,)), dma((3, 5)), dma((3, 5)),
+            dma((3, 8 * PARTS)), dma((3, 8 * PARTS)), dma((3, 8 * PARTS)), dma((3, 8 * PARTS)),
         ],
         compiler_params=pltpu.CompilerParams(
-            has_side_effects=True, vmem_limit_bytes=50 * 1024 * 1024
+            collective_id=0, has_side_effects=True, vmem_limit_bytes=50 * 1024 * 1024
         ),
         cost_estimate=pl.CostEstimate(flops=8 * 10**9, bytes_accessed=3 * 10**6, transcendentals=10**6),
     )(latents, norm_gain, norm_shift, conv_weight, conv_bias)

time: 142 us -> 125 us (0.88)
  Pallas kernels: 135 us -> 118 us
    pallas_call x1, Pallas kernels: 135 us -> 118 us  [on_device(): pl.pallas_call(kernel, out_shape=jax.ShapeDtypeStruct((2, 2, 32, 512), BF...]
where the time goes in v2:
time: 125 us; the launch traced here: 123 us
  Pallas kernels  118 us (94%)
  local copies, waits for them, and re-layouts  5.38 us (4%)
    pallas_call x1, Pallas kernels, on_device(): pl.pallas_call(kernel, out_shape=jax.ShapeDtypeStruct((2, 2, 32, 512), BF...  118 us
    unnamed x11, local copies, waits for them, and re-layouts  5.38 us

profile of v2, /device:TPU:3, one launch (start us, length us, event | category | flops | bytes accessed | tf_op | source)
XLA Modules:
  0.0 123.3 jit_solution(7318200457001073382)
XLA Ops:
  0.0 0.0 copy-start
  0.0 1.7 %copy-done = bf16[3,27,32,512]{3,2,1,0:T(8,128)(2,1)S(1)} copy-done((bf16[3,27,32,512]{3,2,1,0:T(8,128)(2,1)S(1)}, bf16[3,27,32,512]{3,2,1,0:T(8,128)(2,1)}, u32[]{:S(2)}) %copy-start) | copy-done | bytes 2654232
  1.8 0.0 copy-start.1
  1.8 0.9 copy-done.1
  2.7 0.0 copy-start.2
  2.7 0.7 copy-done.2
  3.4 0.0 copy-start.3
  3.4 0.7 copy-done.3
  4.0 0.0 copy-start.4
  4.1 0.7 copy-done.4
  4.7 117.9 %shard_map.55 = bf16[2,2,32,512]{3,2,1,0:T(8,128)(2,1)S(1)} custom-call(bf16[2,2,32,512]{3,2,1,0:T(8,128)(2,1)S(1)} %copy-done.1, f32[3,512]{1,0:T(4,128)S(1)} %copy-done.2, f32[3,512]{1,0:T(4,128)S(1)} %copy-done.3, bf16[3,27,32,512]{3,2,1,0:T(8,128)(2,1)S(1)} %copy-done, f32[3,32]{1,0:T(4,128)S(1)} %copy-done.4), custom_call_target="tpu_custom_call" | custom-call | flops 8000000000 | bytes 3000000 | tf_op jit(solution)/shard_map/pallas_call | solution.py:452
  122.7 0.7 copy.7
Async XLA Ops:
  0.0 1.7 %copy-start = (bf16[3,27,32,512]{3,2,1,0:T(8,128)(2,1)S(1)}, bf16[3,27,32,512]{3,2,1,0:T(8,128)(2,1)}, u32[]{:S(2)}) copy-start(bf16[3,27,32,512]{3,2,1,0:T(8,128)(2,1)} %w_hbm.1) | copy-start | bytes 7962628
  1.8 0.9 copy-start.1
  2.7 0.7 copy-start.2
  3.4 0.7 copy-start.3
  4.0 0.7 copy-start.4

commit v3 on v2

v3 whole, which is shorter than its diff:
```python
import jax
import jax.numpy as jnp
from jax import lax
from jax.experimental import pallas as pl
from jax.experimental.pallas import tpu as pltpu
from jax.sharding import PartitionSpec as P

MESH = pl.DeviceIdType.MESH
BF, F32 = jnp.bfloat16, jnp.float32
EPSILON = 1e-06
LAYERS = 3
MAIN = 10 * 256
TOP = MAIN
BOT = MAIN + 256
PREV = MAIN + 512
LANES = MAIN + 640
SENT = LANES - 512
PARTS = ((0, 1024), (1024, 2048), (2048, SENT))
PER_FRAME = 32 * 32 * 16


def lane_of(shape):
    return lax.broadcasted_iota(jnp.int32, shape, len(shape) - 1)


def roll(x, shift):
    size = x.shape[-1]
    shift = shift % size
    return x if shift == 0 else pltpu.roll(x, shift, axis=x.ndim - 1)


def silu(v):
    half = 0.5 * v
    return half + half * jnp.tanh(half)


def kernel(
    lat_hbm, gain_hbm, shift_hbm, w_hbm, bias_hbm, out_ref,
    lat_ref, gain_ref, shift_ref, bias_ref,
    w_ref, local_t, slots_in, raw, before, own, top_out, bot_out, top_in, bot_in, top_prev, bot_prev,
    stat_out, stat_in, mask_ref, coef, y_ref, slots_out, final_t, par_ref, column_ref, bias_col,
    in_sem, w_sem, a2a_send, a2a_recv, fin_send, fin_recv, stat_send, stat_recv, coef_send, coef_recv,
    halo_send, halo_recv, later_send, later_recv, ring_send, ring_recv, sib_send, sib_recv,
):
    tm = lax.axis_index("tm")
    tile = lax.axis_index("tile")
    x, y = lax.rem(tm, 4), lax.div(tm, 4)
    z, core = lax.div(tile, 2), lax.rem(tile, 2)
    chans = pl.multiple_of(tile * 32, 32)
    sibling = z * 2 + (1 - core)
    right = lax.rem(z + 1, 8) * 2 + core
    left = lax.rem(z + 7, 8) * 2 + core

    def remote(src, dst, send, recv, to_tm, to_tile):
        return pltpu.make_async_remote_copy(
            src_ref=src, dst_ref=dst, send_sem=send, recv_sem=recv,
            device_id=(to_tm, to_tile), device_id_type=MESH,
        )

    load_w = pltpu.make_async_copy(w_hbm, w_ref, w_sem)
    loads = [
        pltpu.make_async_copy(src, dst, in_sem.at[i])
        for i, (src, dst) in enumerate((
            (lat_hbm, lat_ref), (gain_hbm, gain_ref), (shift_hbm, shift_ref), (bias_hbm, bias_ref),
        ))
    ]
    for load in loads:
        load.start()
    load_w.start()

    barrier = pltpu.get_barrier_semaphore()
    own_x = lax.div(tile, 4) == x

    def greet(to_tm, to_tile):
        pl.semaphore_signal(barrier, inc=1, device_id=(to_tm, to_tile), device_id_type=MESH)

    def greet_tm(k, c):
        greet(lax.rem(tm + k, 16), tile)
        return c

    def greet_a2a(k, c):
        to_tm = y * 4 + lax.div(tile, 4)

        @pl.when(jnp.logical_not(jnp.logical_and(to_tm == tm, k == tile)))
        def _():
            greet(to_tm, k)

        from_tm, from_tile = y * 4 + lax.div(k, 4), x * 4 + lax.rem(k, 4)

        @pl.when(jnp.logical_not(jnp.logical_and(from_tm == tm, from_tile == tile)))
        def _():
            greet(from_tm, from_tile)

        return c

    lax.fori_loop(0, 16, greet_a2a, 0)
    lax.fori_loop(1, 16, greet_tm, 0)
    greet(tm, sibling)
    for k in range(1, 8):
        greet(tm, lax.rem(z + k, 8) * 2 + core)

    loads[0].wait()
    mine = lat_ref[...].reshape(128, 512).astype(F32)
    local_t[...] = mine.T.astype(BF)
    my_slot = x * 4 + lax.rem(tile, 4)

    def in_copy(t):
        return remote(
            local_t.at[pl.ds(pl.multiple_of(t * 32, 32), 32)], slots_in.at[my_slot],
            a2a_send, a2a_recv, y * 4 + lax.div(tile, 4), t,
        )

    def send_in(t, carry):
        to_self = jnp.logical_and(t == tile, own_x)

        @pl.when(to_self)
        def _():
            pltpu.make_async_copy(
                local_t.at[pl.ds(pl.multiple_of(t * 32, 32), 32)], slots_in.at[my_slot], a2a_recv
            ).start()

        @pl.when(jnp.logical_not(to_self))
        def _():
            in_copy(t).start()

        return carry

    pl.semaphore_wait(barrier, jnp.where(own_x, 53, 55))
    lax.fori_loop(0, 16, send_in, 0)

    for load in loads[1:]:
        load.wait()
    par_ref[...] = jnp.zeros_like(par_ref)
    par_ref[0:3, :] = gain_ref[...]
    par_ref[3:6, :] = shift_ref[...]
    columns = jnp.concatenate([par_ref[...], jnp.zeros((120, 512), F32)], axis=0)
    column_ref[...] = columns.T.reshape(8, 2, 32, 128)
    par_ref[...] = jnp.zeros_like(par_ref)
    par_ref[0:3, 0:32] = bias_ref[...]
    columns = jnp.concatenate([par_ref[:, 0:128], jnp.zeros((120, 128), F32)], axis=0)
    bias_col[...] = columns.T[0:32]

    def column(table, index):
        return jnp.sum(jnp.where(lane_of((32, 128)) == index, table, 0.0), axis=1, keepdims=True)

    mask_lane = lax.broadcasted_iota(jnp.int32, (128, 128), 0)
    mask_col = lax.broadcasted_iota(jnp.int32, (128, 128), 1)
    wanted = jnp.maximum(8 * y - 2 + lax.rem(mask_col, 16), 0)
    fits = (mask_lane < 16) & (mask_col < 32) & (lax.div(mask_lane, 8) == lax.div(mask_col, 16))
    for q in range(4):
        mask_ref[q] = jnp.where(fits & (8 * q + lax.rem(mask_lane, 8) <= wanted), 1.0, 0.0)

    pltpu.make_async_copy(slots_in, slots_in, a2a_recv).wait()
    lane128 = lane_of((32, 128))
    for part in range(4):
        for block in range(2):
            one = slots_in[part * 4 + 2 * block].astype(F32)
            two = slots_in[part * 4 + 2 * block + 1].astype(F32)
            for inner in range(2):
                if inner == 0:
                    frame = jnp.where(lane128 < 64, one, roll(two, 64))
                else:
                    frame = jnp.where(lane128 < 64, roll(one, 64), two)
                at = 256 * (2 * part + inner) + 128 * block
                frame = frame.astype(BF)
                raw[0, z, :, at:at + 128] = frame
                own[:, at:at + 128] = frame

    lane256 = lane_of((32, 256))
    col256, row256 = lax.rem(lane256, 32), lax.div(lane256, 32)

    def ring_copy(layer, way, step, part):
        owner = lax.rem(z + 8 + ((1 - step) if way == 0 else (step - 1)), 8)
        piece = raw.at[layer, owner, :, slice(*PARTS[part])]
        at = (way * 4 + step - 1) * 3 + part
        return remote(
            piece, piece, ring_send.at[layer, at], ring_recv.at[layer, at], tm, right if way == 0 else left
        )

    ring_order = [
        (way, step, part)
        for step in range(1, 5) for part in range(3) for way in (0, 1)
        if step < 4 or (part == 1) == (way == 1)
    ]

    def later_copy(layer, owner):
        return remote(
            raw.at[layer, owner, :, 1536:2048], before.at[layer, owner],
            later_send.at[layer, owner], later_recv.at[layer, owner], lax.rem(y + 1, 4) * 4 + x, tile,
        )

    def sib_copy(layer, owner, kind):
        piece = y_ref.at[layer, owner, core, :, slice(*((512, LANES), (0, 512))[kind])]
        return remote(
            piece, piece, sib_send.at[layer, kind, owner], sib_recv.at[layer, kind, owner], tm, sibling
        )

    def coef_copy(layer, k):
        to = lax.rem(z + k, 8) * 2 + core
        return remote(
            coef.at[layer, z], coef.at[layer, z], coef_send.at[layer], coef_recv.at[layer], tm, to
        )

    def halo_copies(layer):
        to_left, to_right = lax.rem(x + 3, 4), lax.rem(x + 1, 4)
        later = lax.rem(y + 1, 4)
        plan = [
            (top_out, bot_in, y * 4 + to_left), (bot_out, top_in, y * 4 + to_right),
            (top_out, bot_prev, later * 4 + to_left), (bot_out, top_prev, later * 4 + to_right),
        ]
        copies = [
            remote(src.at[layer], dst.at[layer], halo_send.at[layer, i], halo_recv.at[layer, i], to, tile)
            for i, (src, dst, to) in enumerate(plan)
        ]
        return copies

    def stat_copy(layer, k):
        other = lax.rem(tm + k, 16)
        return remote(
            stat_out.at[layer], stat_in.at[layer, 15 - k], stat_send.at[layer], stat_recv.at[layer], other, tile
        )

    slot128 = lax.div(lane128, 32)
    low_half = lax.broadcasted_iota(jnp.int32, (32, 128), 0) < 16
    opening = y == 0

    def coefficients(layer, owner):
        table = coef[layer, owner]
        table = jnp.where(low_half, table[0:1], table[1:2])
        columns = column_ref[owner, core]
        scaled = table * column(columns, layer)
        return table, scaled, column(columns, 3 + layer)

    def normal_own(layer, owner):
        average, scaled, shift = coefficients(layer, owner)
        for f in range(8):
            j = f + 2
            values = raw[layer, owner, :, 256 * f:256 * f + 256].astype(F32)
            values = (values - average[:, j:j + 1]) * scaled[:, 16 + j:17 + j] + shift
            y_ref[layer, owner, core, :, 256 * j:256 * j + 256] = silu(values).astype(BF)
        for b in range(5):
            if b == 4:
                frames = (0, 1, 0, 1)
                outside = (slot128 < 2) & (x == 0) | (slot128 >= 2) & (x == 3)
            else:
                frames = [b % 2 + 2 + 2 * s for s in range(4)]
                outside = (x == 0) if b < 2 else (x == 3)
            at = 2048 + 128 * b
            values = raw[layer, owner, :, at:at + 128].astype(F32)
            average_at, scaled_at = average[:, frames[0]:frames[0] + 1], scaled[:, 16 + frames[0]:17 + frames[0]]
            for s in range(1, 4):
                j = frames[s]
                average_at = jnp.where(slot128 == s, average[:, j:j + 1], average_at)
                scaled_at = jnp.where(slot128 == s, scaled[:, 16 + j:17 + j], scaled_at)
            values = jnp.where(outside, 0.0, silu((values - average_at) * scaled_at + shift))
            y_ref[layer, owner, core, :, MAIN + 128 * b:MAIN + 128 * b + 128] = values.astype(BF)
        sib_copy(layer, owner, 0).start()

    def normal_before(layer, owner):
        average, scaled, shift = coefficients(layer, owner)
        for j in range(2):
            values = before[layer, owner, :, 256 * j:256 * j + 256].astype(F32)
            values = jnp.where(opening, raw[layer, owner, :, 0:256].astype(F32), values)
            values = (values - average[:, j:j + 1]) * scaled[:, 16 + j:17 + j] + shift
            y_ref[layer, owner, core, :, 256 * j:256 * j + 256] = silu(values).astype(BF)
        sib_copy(layer, owner, 1).start()

    def layer_step(layer, carry):
        for part in range(2):
            for way in (0, 1):
                ring_copy(layer, way, 1, part).start()
        later_copy(layer, z).start()
        halos = halo_copies(layer)
        sums = jnp.zeros((32, 128), F32)
        tops = [jnp.zeros((32, 128), F32)] * 2
        bots = [jnp.zeros((32, 128), F32)] * 2
        for f in range(8):
            values = own[:, 256 * f:256 * f + 256].astype(F32)
            first = jnp.sum(values, axis=1, keepdims=True)
            second = jnp.sum(values * values, axis=1, keepdims=True)
            sums = jnp.where(lane128 == f, first, sums)
            sums = jnp.where(lane128 == 8 + f, second, sums)
            slot = f // 2
            here = lax.div(lane128, 32) == slot
            tops[f % 2] = jnp.where(here, roll(values[:, :128], 32 * slot), tops[f % 2])
            bots[f % 2] = jnp.where(here, roll(values[:, 128:], 32 * slot - 96), bots[f % 2])
        for i in range(2):
            top_out[layer, :, 128 * i:128 * i + 128] = tops[i].astype(BF)
            bot_out[layer, :, 128 * i:128 * i + 128] = bots[i].astype(BF)
        low = jnp.sum(sums[0:16], axis=0, keepdims=True)
        high = jnp.sum(sums[16:32], axis=0, keepdims=True)
        sub8 = lax.broadcasted_iota(jnp.int32, (8, 128), 0)
        stat_out[layer] = jnp.where(sub8 == 0, low, jnp.where(sub8 == 1, high, 0.0))

        for copy in halos:
            copy.start()

        def send_stat(k, c):
            stat_copy(layer, k).start()
            return c

        lax.fori_loop(1, 16, send_stat, 0)

        for copy in halos:
            copy.wait_recv()
        raw[layer, z, :, 2048:2304] = top_in[layer]
        raw[layer, z, :, 2304:2560] = bot_in[layer]
        values = jnp.zeros((32, 128), F32)
        for i, (now, earlier) in enumerate(((top_in, top_prev), (bot_in, bot_prev))):
            first = now[layer, :, 0:128].astype(F32)
            for b in range(2):
                last = earlier[layer, :, 128 * b:128 * b + 128].astype(F32)
                slot = 2 * i + b
                moved = jnp.where(opening, roll(first, 32 * slot), roll(last, 32 * slot - 96))
                values = jnp.where(slot128 == slot, moved, values)
        raw[layer, z, :, 2560:2688] = values.astype(BF)
        for way in (0, 1):
            ring_copy(layer, way, 1, 2).start()

        def pass_on(at_step):
            for way, step, part in ring_order:
                if step == at_step:
                    ring_copy(layer, way, step, part).wait_recv()
                    if (way, step + 1, part) in ring_order:
                        ring_copy(layer, way, step + 1, part).start()
                    if part == 1:
                        owner = lax.rem(z + 8 + (-step if way == 0 else step), 8)
                        later_copy(layer, owner).start()

        pass_on(1)

        pltpu.make_async_copy(stat_in.at[layer], stat_in.at[layer], stat_recv.at[layer]).wait()
        sources = [jnp.zeros((8, 128), F32)] * 4
        for s in range(16):
            block = stat_out[layer] if s == 15 else stat_in[layer, s]
            from_y = lax.div(lax.rem(tm + 16 - (15 - s), 16), 4)
            for q in range(4):
                sources[q] = sources[q] + jnp.where(from_y == q, block, 0.0)
        cumulative = jnp.zeros((8, 128), F32)
        for q in range(4):
            cumulative = cumulative + lax.dot_general(
                sources[q], mask_ref[q], (((1,), (0,)), ((), ())),
                precision=lax.Precision.HIGHEST, preferred_element_type=F32,
            )
        lane8 = lane_of((8, 128))
        count = ((jnp.maximum(8 * y - 2 + lax.rem(lane8, 16), 0) + 1) * PER_FRAME).astype(F32)
        average = cumulative / count
        spread = roll(average, -16)
        inverse = lax.rsqrt(spread - average * average + EPSILON)
        coef[layer, z] = jnp.where(lane8 < 16, average, roll(inverse, 16))
        for k in range(1, 8):
            coef_copy(layer, k).start()
        normal_own(layer, z)
        pass_on(2)
        pltpu.make_async_copy(coef.at[layer, 0:7], coef.at[layer, 0:7], coef_recv.at[layer]).wait()

        def both(work):
            def one(way, c):
                work(way)
                return c

            lax.fori_loop(0, 2, one, 0)

        def at_distance(step):
            return lambda way: lax.rem(z + 8 + (1 - 2 * way) * step, 8)

        def own_rows(step):
            owner = at_distance(step)
            both(lambda way: normal_own(layer, owner(way)))

        def rows_before(step):
            owner = at_distance(step)

            def work(way):
                later_copy(layer, owner(way)).wait_recv()
                normal_before(layer, owner(way))

            both(work)

        own_rows(1)
        pass_on(3)
        own_rows(2)
        later_copy(layer, z).wait_recv()
        normal_before(layer, z)
        rows_before(1)
        pass_on(4)
        own_rows(3)
        far = lax.rem(z + 4, 8)
        normal_own(layer, far)
        rows_before(2)
        rows_before(3)
        later_copy(layer, far).wait_recv()
        normal_before(layer, far)

        def from_sibling(owner, c):
            for kind in range(2):
                piece = y_ref.at[layer, owner, 1 - core, :, slice(*((512, LANES), (0, 512))[kind])]
                pltpu.make_async_copy(piece, piece, sib_recv.at[layer, kind, owner]).wait()
            return c

        lax.fori_loop(0, 8, from_sibling, 0)

        @pl.when(layer == 0)
        def _():
            load_w.wait()

        def product(first_offset, count, lanes_at):
            total = None
            for dt in range(3):
                matrix = w_ref[layer, pl.ds(9 * dt + first_offset, count)].reshape(32 * count, 512)
                cells = y_ref[layer, :, :, :, lanes_at(dt)].reshape(512, 256)
                term = lax.dot_general(
                    matrix, cells, (((1,), (0,)), ((), ())), preferred_element_type=F32
                )
                total = term if total is None else total + term
            return total

        def across(total):
            before = jnp.where(col256 >= 1, roll(total[0:32], 1), 0.0)
            after = jnp.where(col256 <= 30, roll(total[64:96], -1), 0.0)
            return before + total[32:64] + after

        def edge_rows(base, first_offset, slot):
            early, late, now = [
                lax.dot_general(
                    w_ref[layer, pl.ds(9 * dt + first_offset, 3)].reshape(96, 512),
                    y_ref[layer, :, :, :, base:base + 256].reshape(512, 256),
                    (((1,), (0,)), ((), ())), preferred_element_type=F32,
                )
                for dt in range(3)
            ]
            before, middle = [
                lax.dot_general(
                    w_ref[layer, pl.ds(9 * dt + first_offset, 3)].reshape(96, 512),
                    y_ref[layer, :, :, :, PREV:PREV + 128].reshape(512, 128),
                    (((1,), (0,)), ((), ())), preferred_element_type=F32,
                )
                for dt in range(2)
            ]
            slots = lax.div(lane_of((96, 128)), 32)
            even = roll(early[:, :128] + late[:, 128:], 32)
            odd = roll(early[:, 128:], 32)
            even = jnp.where(slots == 0, roll(before, -32 * slot) + roll(middle, -32 * slot - 32), even)
            odd = jnp.where(slots == 0, roll(before, -32 * slot - 32), odd)
            even = even + now[:, :128]
            odd = odd + late[:, :128] + now[:, 128:]
            return across(jnp.concatenate([even, odd], axis=1))

        upper = edge_rows(TOP, 0, 0)
        lower = edge_rows(BOT, 6, 2)
        bias = column(bias_col[...], layer)
        keep = jnp.where(layer == 1, 1.0, 0.0)
        for f in range(8):
            total = product(0, 9, lambda dt: slice(256 * (f + dt), 256 * (f + dt) + 256))
            above = roll(across(total[0:96]), 32)
            below = roll(across(total[192:288]), -32)
            slot = f // 2
            edge = 128 * (f % 2)
            from_upper = roll(upper[:, edge:edge + 128], -32 * slot)
            from_lower = roll(lower[:, edge:edge + 128], 96 - 32 * slot)
            zero = jnp.zeros((32, 128), F32)
            above = jnp.where(row256 == 0, jnp.concatenate([from_upper, zero], axis=1), above)
            below = jnp.where(row256 == 7, jnp.concatenate([zero, from_lower], axis=1), below)
            result = above + across(total[96:192]) + below + bias
            here = slice(256 * f, 256 * f + 256)
            result = result + keep * raw[0, z, :, here].astype(F32)
            result = result.astype(BF)
            own[:, here] = result

            @pl.when(layer + 1 < LAYERS)
            def _():
                raw[layer + 1, z, :, here] = result

        return carry

    lax.fori_loop(0, LAYERS, layer_step, 0)

    for part in range(4):
        for block in range(2):
            at = 512 * part + 128 * block
            one = own[:, at:at + 128].astype(F32)
            two = own[:, at + 256:at + 384].astype(F32)
            slots_out[part * 4 + 2 * block] = jnp.where(lane128 < 64, one, roll(two, 64)).astype(BF)
            slots_out[part * 4 + 2 * block + 1] = jnp.where(lane128 < 64, roll(one, 64), two).astype(BF)

    def send_out(slot, c):
        to_tm = y * 4 + lax.div(slot, 4)
        to_tile = x * 4 + lax.rem(slot, 4)
        to_self = jnp.logical_and(to_tm == tm, to_tile == tile)
        rows = final_t.at[pl.ds(chans, 32)]

        @pl.when(to_self)
        def _():
            pltpu.make_async_copy(slots_out.at[slot], rows, fin_recv).start()

        @pl.when(jnp.logical_not(to_self))
        def _():
            remote(slots_out.at[slot], rows, fin_send, fin_recv, to_tm, to_tile).start()

        return c

    lax.fori_loop(0, 16, send_out, 0)
    pltpu.make_async_copy(final_t, final_t, fin_recv).wait()
    out_ref[...] = final_t[...].astype(F32).T.astype(BF).reshape(2, 2, 32, 512)


    def sent(ref, sem):
        @pl.when(own_x)
        def _():
            pltpu.make_async_copy(ref.at[0:15], ref.at[0:15], sem).wait()

        @pl.when(jnp.logical_not(own_x))
        def _():
            pltpu.make_async_copy(ref, ref, sem).wait()

    sent(slots_in, a2a_send)
    sent(slots_out, fin_send)

    def drain(layer, c):
        for copy in halo_copies(layer):
            copy.wait_send()
        pltpu.make_async_copy(stat_in.at[layer], stat_in.at[layer], stat_send.at[layer]).wait()
        pltpu.make_async_copy(coef.at[layer, 0:7], coef.at[layer, 0:7], coef_send.at[layer]).wait()
        for entry in ring_order:
            ring_copy(layer, *entry).wait_send()

        def drain_owner(owner, carry):
            later_copy(layer, owner).wait_send()
            for kind in range(2):
                sib_copy(layer, owner, kind).wait_send()
            return carry

        lax.fori_loop(0, 8, drain_owner, 0)
        return c

    lax.fori_loop(0, LAYERS, drain, 0)


def on_device(latents, norm_gain, norm_shift, conv_weight, conv_bias):
    vmem = pl.BlockSpec(memory_space=pltpu.VMEM)
    dma = pltpu.SemaphoreType.DMA
    return pl.pallas_call(
        kernel,
        out_shape=jax.ShapeDtypeStruct((2, 2, 32, 512), BF),
        in_specs=[pl.BlockSpec(memory_space=pltpu.HBM)] * 5,
        out_specs=vmem,
        scratch_shapes=[
            pltpu.VMEM((2, 2, 32, 512), BF),
            pltpu.VMEM((3, 512), F32),
            pltpu.VMEM((3, 512), F32),
            pltpu.VMEM((3, 32), F32),
            pltpu.VMEM((3, 27, 32, 512), BF),
            pltpu.VMEM((512, 128), BF),
            pltpu.VMEM((16, 32, 128), BF),
            pltpu.VMEM((3, 8, 32, SENT), BF),
            pltpu.VMEM((3, 8, 32, 512), BF),
            pltpu.VMEM((32, 2048), BF),
            pltpu.VMEM((3, 32, 256), BF),
            pltpu.VMEM((3, 32, 256), BF),
            pltpu.VMEM((3, 32, 256), BF),
            pltpu.VMEM((3, 32, 256), BF),
            pltpu.VMEM((3, 32, 256), BF),
            pltpu.VMEM((3, 32, 256), BF),
            pltpu.VMEM((3, 8, 128), F32),
            pltpu.VMEM((3, 15, 8, 128), F32),
            pltpu.VMEM((4, 128, 128), F32),
            pltpu.VMEM((3, 8, 8, 128), F32),
            pltpu.VMEM((3, 8, 2, 32, LANES), BF),
            pltpu.VMEM((16, 32, 128), BF),
            pltpu.VMEM((512, 128), BF),
            pltpu.VMEM((8, 512), F32),
            pltpu.VMEM((8, 2, 32, 128), F32),
            pltpu.VMEM((32, 128), F32),
            dma((4,)), dma, dma, dma, dma, dma, dma((3,)), dma((3,)), dma((3,)), dma((3,)),
            dma((3, 4)), dma((3, 4)), dma((3, 8)), dma((3, 8)),
            dma((3, 24)), dma((3, 24)), dma((3, 2, 8)), dma((3, 2, 8)),
        ],
        compiler_params=pltpu.CompilerParams(
            collective_id=0, has_side_effects=True, vmem_limit_bytes=64 * 1024 * 1024
        ),
        cost_estimate=pl.CostEstimate(flops=8 * 10**9, bytes_accessed=3 * 10**6, transcendentals=10**6),
    )(latents, norm_gain, norm_shift, conv_weight, conv_bias)


def solution(mesh):
    placed = (P("tm", "tile", None, None), P(), P(), P(None, None, "tile", None), P(None, "tile"))
    return jax.shard_map(
        on_device,
        mesh=mesh,
        in_specs=placed,
        out_specs=P("tm", "tile", None, None),
        check_vma=False,
    )
```

time: 125 us -> 122 us (0.976)
  local copies, waits for them, and re-layouts: 5.38 us -> 1.57 us
    unnamed x11 -> x1, local copies, waits for them, and re-layouts: 5.38 us -> 1.57 us
    pallas_call x1, Pallas kernels: 118 us -> 119 us  [on_device(): pl.pallas_call(kernel, out_shape=jax.ShapeDtypeStruct((2, 2, 32, 512), BF...]
where the time goes in v3:
time: 122 us; the launch traced here: 121 us
  Pallas kernels  119 us (98%)
  local copies, waits for them, and re-layouts  1.57 us (1%)
    pallas_call x1, Pallas kernels, on_device(): pl.pallas_call(kernel, out_shape=jax.ShapeDtypeStruct((2, 2, 32, 512), BF...  119 us

profile of v3, /device:TPU:3, one launch (start us, length us, event | category | flops | bytes accessed | tf_op | source)
XLA Modules:
  0.0 120.9 jit_solution(3141129645914038219)
XLA Ops:
  0.0 119.3 %shard_map.55 = bf16[2,2,32,512]{3,2,1,0:T(8,128)(2,1)} custom-call(bf16[2,2,32,512]{3,2,1,0:T(8,128)(2,1)} %lat_hbm.1, f32[3,512]{1,0:T(4,128)} %gain_hbm.1, f32[3,512]{1,0:T(4,128)} %shift_hbm.1, bf16[3,27,32,512]{3,2,1,0:T(8,128)(2,1)} %w_hbm.1, f32[3,32]{1,0:T(4,128)} %bias_hbm.1), custom_call_target="tpu_custom_call" | custom-call | flops 8000000000 | bytes 3000000 | tf_op jit(solution)/shard_map/pallas_call | solution.py:542
  119.4 1.6 %copy.7 = bf16[2,2,32,512]{3,2,1,0:T(8,128)(2,1)} copy(bf16[2,2,32,512]{3,2,1,0:T(8,128)(2,1)} %shard_map.55) | data formatting | bytes 262144

commit v4 on v3

--- a/solution.py
+++ b/solution.py
@@ -37,9 +37,9 @@
 def kernel(
     lat_hbm, gain_hbm, shift_hbm, w_hbm, bias_hbm, out_ref,
     lat_ref, gain_ref, shift_ref, bias_ref,
-    w_ref, local_t, slots_in, raw, before, own, top_out, bot_out, top_in, bot_in, top_prev, bot_prev,
-    stat_out, stat_in, mask_ref, coef, y_ref, slots_out, final_t, par_ref, column_ref, bias_col,
-    in_sem, w_sem, a2a_send, a2a_recv, fin_send, fin_recv, stat_send, stat_recv, coef_send, coef_recv,
+    w_ref, local_t, slots_in, raw, before, top_out, bot_out, top_in, bot_in, top_prev, bot_prev,
+    stat_out, stat_in, mask_ref, coef, y_ref, slots_out, mid, final_t, par_ref, column_ref, bias_col, table_ref, wk_ref, part_ref,
+    in_sem, w_sem, a2a_send, a2a_recv, mid_send, mid_recv, fin_send, fin_recv, stat_send, stat_recv, coef_send, coef_recv,
     halo_send, halo_recv, later_send, later_recv, ring_send, ring_recv, sib_send, sib_recv,
 ):
     tm = lax.axis_index("tm")
@@ -79,12 +79,6 @@
         return c
 
     def greet_a2a(k, c):
-        to_tm = y * 4 + lax.div(tile, 4)
-
-        @pl.when(jnp.logical_not(jnp.logical_and(to_tm == tm, k == tile)))
-        def _():
-            greet(to_tm, k)
-
         from_tm, from_tile = y * 4 + lax.div(k, 4), x * 4 + lax.rem(k, 4)
 
         @pl.when(jnp.logical_not(jnp.logical_and(from_tm == tm, from_tile == tile)))
@@ -93,11 +87,13 @@
 
         return c
 
+    def greet_tile(k, c):
+        greet(tm, lax.rem(tile + k, 16))
+        return c
+
     lax.fori_loop(0, 16, greet_a2a, 0)
     lax.fori_loop(1, 16, greet_tm, 0)
-    greet(tm, sibling)
-    for k in range(1, 8):
-        greet(tm, lax.rem(z + k, 8) * 2 + core)
+    lax.fori_loop(1, 16, greet_tile, 0)
 
     loads[0].wait()
     mine = lat_ref[...].reshape(128, 512).astype(F32)
@@ -125,7 +121,7 @@
 
         return carry
 
-    pl.semaphore_wait(barrier, jnp.where(own_x, 53, 55))
+    pl.semaphore_wait(barrier, jnp.where(own_x, 45, 46))
     lax.fori_loop(0, 16, send_in, 0)
 
     for load in loads[1:]:
@@ -143,6 +139,14 @@
     def column(table, index):
         return jnp.sum(jnp.where(lane_of((32, 128)) == index, table, 0.0), axis=1, keepdims=True)
 
+    def spread(owner, c):
+        columns = column_ref[owner, core]
+        for i in range(6):
+            table_ref[i, owner] = jnp.broadcast_to(column(columns, i), (32, 128))
+        return c
+
+    lax.fori_loop(0, 8, spread, 0)
+
     mask_lane = lax.broadcasted_iota(jnp.int32, (128, 128), 0)
     mask_col = lax.broadcasted_iota(jnp.int32, (128, 128), 1)
     wanted = jnp.maximum(8 * y - 2 + lax.rem(mask_col, 16), 0)
@@ -150,8 +154,63 @@
     for q in range(4):
         mask_ref[q] = jnp.where(fits & (8 * q + lax.rem(mask_lane, 8) <= wanted), 1.0, 0.0)
 
+    lane128 = lane_of((32, 128))
+    slot128 = lax.div(lane128, 32)
+
+    def send_frames(part):
+        for block in range(2):
+            at = 512 * part + 128 * block
+            one = raw[LAYERS, z, :, at:at + 128].astype(F32)
+            two = raw[LAYERS, z, :, at + 256:at + 384].astype(F32)
+            slots_out[part, 2 * block] = jnp.where(lane128 < 64, one, roll(two, 64)).astype(BF)
+            slots_out[part, 2 * block + 1] = jnp.where(lane128 < 64, roll(one, 64), two).astype(BF)
+
+        @pl.when(x == part)
+        def _():
+            mid[part] = slots_out[part]
+
+        @pl.when(x != part)
+        def _():
+            remote(slots_out.at[part], mid.at[x], mid_send, mid_recv.at[x], y * 4 + part, tile).start()
+
+    def publish(index, frames):
+        sums = jnp.zeros((32, 128), F32)
+        tops = [jnp.zeros((32, 128), F32)] * 2
+        bots = [jnp.zeros((32, 128), F32)] * 2
+        for f in range(7, -1, -1):
+            values = frames(f).astype(BF)
+            raw[index, z, :, 256 * f:256 * f + 256] = values
+            values = values.astype(F32)
+            first = jnp.sum(values, axis=1, keepdims=True)
+            second = jnp.sum(values * values, axis=1, keepdims=True)
+            sums = jnp.where(lane128 == f, first, sums)
+            sums = jnp.where(lane128 == 8 + f, second, sums)
+            slot = f // 2
+            tops[f % 2] = jnp.where(slot128 == slot, roll(values[:, :128], 32 * slot), tops[f % 2])
+            bots[f % 2] = jnp.where(slot128 == slot, roll(values[:, 128:], 32 * slot - 96), bots[f % 2])
+        for i in range(2):
+            top_out[index, :, 128 * i:128 * i + 128] = tops[i].astype(BF)
+            bot_out[index, :, 128 * i:128 * i + 128] = bots[i].astype(BF)
+        low = jnp.sum(sums[0:16], axis=0, keepdims=True)
+        high = jnp.sum(sums[16:32], axis=0, keepdims=True)
+        sub8 = lax.broadcasted_iota(jnp.int32, (8, 128), 0)
+        stat_out[index] = jnp.where(sub8 == 0, low, jnp.where(sub8 == 1, high, 0.0))
+
+    def split_w(at, c):
+        layer, offset = lax.div(at, 27), lax.rem(at, 27)
+        for q in range(2):
+            one = w_ref[layer, offset, :, 256 * q:256 * q + 128].astype(F32)
+            two = w_ref[layer, offset, :, 256 * q + 128:256 * q + 256].astype(F32)
+            first = jnp.where(slot128 == 0, one, roll(one, -32))
+            first = jnp.where(slot128 < 2, first, jnp.where(slot128 == 2, roll(two, 64), roll(two, 32)))
+            second = jnp.where(slot128 == 0, roll(one, -32), roll(one, -64))
+            second = jnp.where(slot128 < 2, second, jnp.where(slot128 == 2, roll(two, 32), two))
+            wk_ref[0, layer, offset, :, 128 * q:128 * q + 128] = first.astype(BF)
+            wk_ref[1, layer, offset, :, 128 * q:128 * q + 128] = second.astype(BF)
+        return c
+
     pltpu.make_async_copy(slots_in, slots_in, a2a_recv).wait()
-    lane128 = lane_of((32, 128))
+    halves = {}
     for part in range(4):
         for block in range(2):
             one = slots_in[part * 4 + 2 * block].astype(F32)
@@ -161,10 +220,8 @@
                     frame = jnp.where(lane128 < 64, one, roll(two, 64))
                 else:
                     frame = jnp.where(lane128 < 64, roll(one, 64), two)
-                at = 256 * (2 * part + inner) + 128 * block
-                frame = frame.astype(BF)
-                raw[0, z, :, at:at + 128] = frame
-                own[:, at:at + 128] = frame
+                halves[2 * part + inner, block] = frame
+    publish(0, lambda f: jnp.concatenate([halves[f, 0], halves[f, 1]], axis=1))
 
     lane256 = lane_of((32, 256))
     col256, row256 = lax.rem(lane256, 32), lax.div(lane256, 32)
@@ -192,13 +249,13 @@
     def sib_copy(layer, owner, kind):
         piece = y_ref.at[layer, owner, core, :, slice(*((512, LANES), (0, 512))[kind])]
         return remote(
-            piece, piece, sib_send.at[layer, kind, owner], sib_recv.at[layer, kind, owner], tm, sibling
+            piece, piece, sib_send.at[layer, kind, owner], sib_recv.at[layer, kind], tm, sibling
         )
 
     def coef_copy(layer, k):
         to = lax.rem(z + k, 8) * 2 + core
         return remote(
-            coef.at[layer, z], coef.at[layer, z], coef_send.at[layer], coef_recv.at[layer], tm, to
+            coef.at[layer, z], coef.at[layer, z], coef_send.at[layer, k], coef_recv.at[layer, k], tm, to
         )
 
     def halo_copies(layer):
@@ -220,23 +277,22 @@
             stat_out.at[layer], stat_in.at[layer, 15 - k], stat_send.at[layer], stat_recv.at[layer], other, tile
         )
 
-    slot128 = lax.div(lane128, 32)
     low_half = lax.broadcasted_iota(jnp.int32, (32, 128), 0) < 16
     opening = y == 0
 
     def coefficients(layer, owner):
         table = coef[layer, owner]
         table = jnp.where(low_half, table[0:1], table[1:2])
-        columns = column_ref[owner, core]
-        scaled = table * column(columns, layer)
-        return table, scaled, column(columns, 3 + layer)
+        scaled = table * table_ref[layer, owner]
+        return table, scaled, table_ref[3 + layer, owner]
 
     def normal_own(layer, owner):
         average, scaled, shift = coefficients(layer, owner)
+        wide = jnp.concatenate([shift, shift], axis=1)
         for f in range(8):
             j = f + 2
             values = raw[layer, owner, :, 256 * f:256 * f + 256].astype(F32)
-            values = (values - average[:, j:j + 1]) * scaled[:, 16 + j:17 + j] + shift
+            values = (values - average[:, j:j + 1]) * scaled[:, 16 + j:17 + j] + wide
             y_ref[layer, owner, core, :, 256 * j:256 * j + 256] = silu(values).astype(BF)
         for b in range(5):
             if b == 4:
@@ -258,48 +314,34 @@
 
     def normal_before(layer, owner):
         average, scaled, shift = coefficients(layer, owner)
+        wide = jnp.concatenate([shift, shift], axis=1)
         for j in range(2):
             values = before[layer, owner, :, 256 * j:256 * j + 256].astype(F32)
             values = jnp.where(opening, raw[layer, owner, :, 0:256].astype(F32), values)
-            values = (values - average[:, j:j + 1]) * scaled[:, 16 + j:17 + j] + shift
+            values = (values - average[:, j:j + 1]) * scaled[:, 16 + j:17 + j] + wide
             y_ref[layer, owner, core, :, 256 * j:256 * j + 256] = silu(values).astype(BF)
         sib_copy(layer, owner, 1).start()
 
     def layer_step(layer, carry):
+        halos = halo_copies(layer)
+        for copy in halos:
+            copy.start()
         for part in range(2):
             for way in (0, 1):
                 ring_copy(layer, way, 1, part).start()
-        later_copy(layer, z).start()
-        halos = halo_copies(layer)
-        sums = jnp.zeros((32, 128), F32)
-        tops = [jnp.zeros((32, 128), F32)] * 2
-        bots = [jnp.zeros((32, 128), F32)] * 2
-        for f in range(8):
-            values = own[:, 256 * f:256 * f + 256].astype(F32)
-            first = jnp.sum(values, axis=1, keepdims=True)
-            second = jnp.sum(values * values, axis=1, keepdims=True)
-            sums = jnp.where(lane128 == f, first, sums)
-            sums = jnp.where(lane128 == 8 + f, second, sums)
-            slot = f // 2
-            here = lax.div(lane128, 32) == slot
-            tops[f % 2] = jnp.where(here, roll(values[:, :128], 32 * slot), tops[f % 2])
-            bots[f % 2] = jnp.where(here, roll(values[:, 128:], 32 * slot - 96), bots[f % 2])
-        for i in range(2):
-            top_out[layer, :, 128 * i:128 * i + 128] = tops[i].astype(BF)
-            bot_out[layer, :, 128 * i:128 * i + 128] = bots[i].astype(BF)
-        low = jnp.sum(sums[0:16], axis=0, keepdims=True)
-        high = jnp.sum(sums[16:32], axis=0, keepdims=True)
-        sub8 = lax.broadcasted_iota(jnp.int32, (8, 128), 0)
-        stat_out[layer] = jnp.where(sub8 == 0, low, jnp.where(sub8 == 1, high, 0.0))
-
-        for copy in halos:
-            copy.start()
 
         def send_stat(k, c):
             stat_copy(layer, k).start()
             return c
 
         lax.fori_loop(1, 16, send_stat, 0)
+        later_copy(layer, z).start()
+
+        @pl.when(layer == 0)
+        def _():
+            load_w.wait()
+
+        lax.fori_loop(27 * layer, 27 * layer + 27, split_w, 0)
 
         for copy in halos:
             copy.wait_recv()
@@ -323,9 +365,9 @@
                     ring_copy(layer, way, step, part).wait_recv()
                     if (way, step + 1, part) in ring_order:
                         ring_copy(layer, way, step + 1, part).start()
-                    if part == 1:
-                        owner = lax.rem(z + 8 + (-step if way == 0 else step), 8)
-                        later_copy(layer, owner).start()
+            for way in (0, 1) if at_step < 4 else (1,):
+                owner = lax.rem(z + 8 + (-at_step if way == 0 else at_step), 8)
+                later_copy(layer, owner).start()
 
         pass_on(1)
 
@@ -348,11 +390,10 @@
         spread = roll(average, -16)
         inverse = lax.rsqrt(spread - average * average + EPSILON)
         coef[layer, z] = jnp.where(lane8 < 16, average, roll(inverse, 16))
-        for k in range(1, 8):
+        for k in (1, 7, 2, 6, 3, 5, 4):
             coef_copy(layer, k).start()
         normal_own(layer, z)
         pass_on(2)
-        pltpu.make_async_copy(coef.at[layer, 0:7], coef.at[layer, 0:7], coef_recv.at[layer]).wait()
 
         def both(work):
             def one(way, c):
@@ -366,6 +407,8 @@
 
         def own_rows(step):
             owner = at_distance(step)
+            coef_copy(layer, step).wait_recv()
+            coef_copy(layer, 8 - step).wait_recv()
             both(lambda way: normal_own(layer, owner(way)))
 
         def rows_before(step):
@@ -377,43 +420,43 @@
 
             both(work)
 
+        pass_on(3)
         own_rows(1)
-        pass_on(3)
         own_rows(2)
+        own_rows(3)
         later_copy(layer, z).wait_recv()
         normal_before(layer, z)
         rows_before(1)
+        rows_before(2)
         pass_on(4)
-        own_rows(3)
         far = lax.rem(z + 4, 8)
+        coef_copy(layer, 4).wait_recv()
         normal_own(layer, far)
-        rows_before(2)
-        rows_before(3)
-        later_copy(layer, far).wait_recv()
-        normal_before(layer, far)
-
-        def from_sibling(owner, c):
-            for kind in range(2):
-                piece = y_ref.at[layer, owner, 1 - core, :, slice(*((512, LANES), (0, 512))[kind])]
-                pltpu.make_async_copy(piece, piece, sib_recv.at[layer, kind, owner]).wait()
-            return c
-
-        lax.fori_loop(0, 8, from_sibling, 0)
-
-        @pl.when(layer == 0)
-        def _():
-            load_w.wait()
-
-        def product(first_offset, count, lanes_at):
-            total = None
-            for dt in range(3):
-                matrix = w_ref[layer, pl.ds(9 * dt + first_offset, count)].reshape(32 * count, 512)
-                cells = y_ref[layer, :, :, :, lanes_at(dt)].reshape(512, 256)
-                term = lax.dot_general(
+
+        def from_sibling(kind):
+            piece = y_ref.at[layer, :, 1 - core, :, slice(*((512, LANES), (0, 512))[kind])]
+            pltpu.make_async_copy(piece, piece, sib_recv.at[layer, kind]).wait()
+
+        def product(half, first_offset, count, steps, lanes_at, width):
+            total = []
+            for dt in steps:
+                matrix = wk_ref[half, layer, pl.ds(9 * dt + first_offset, count)].reshape(32 * count, 256)
+                cells = y_ref[layer, :, half, :, lanes_at(dt)].reshape(256, width)
+                total.append(lax.dot_general(
                     matrix, cells, (((1,), (0,)), ((), ())), preferred_element_type=F32
-                )
-                total = term if total is None else total + term
+                ))
             return total
+
+        def frame_product(half, f):
+            one, two, three = product(
+                half, 0, 9, range(3), lambda dt: slice(256 * (f + dt), 256 * (f + dt) + 256), 256
+            )
+            return one + two + three
+
+        def edge_products(half, base, first_offset):
+            return product(half, first_offset, 3, range(3), lambda dt: slice(base, base + 256), 256) + product(
+                half, first_offset, 3, range(2), lambda dt: slice(PREV, PREV + 128), 128
+            )
 
         def across(total):
             before = jnp.where(col256 >= 1, roll(total[0:32], 1), 0.0)
@@ -421,21 +464,10 @@
             return before + total[32:64] + after
 
         def edge_rows(base, first_offset, slot):
-            early, late, now = [
-                lax.dot_general(
-                    w_ref[layer, pl.ds(9 * dt + first_offset, 3)].reshape(96, 512),
-                    y_ref[layer, :, :, :, base:base + 256].reshape(512, 256),
-                    (((1,), (0,)), ((), ())), preferred_element_type=F32,
+            early, late, now, before, middle = [
+                mine + theirs for mine, theirs in zip(
+                    mine_edges[base], edge_products(1 - core, base, first_offset), strict=True
                 )
-                for dt in range(3)
-            ]
-            before, middle = [
-                lax.dot_general(
-                    w_ref[layer, pl.ds(9 * dt + first_offset, 3)].reshape(96, 512),
-                    y_ref[layer, :, :, :, PREV:PREV + 128].reshape(512, 128),
-                    (((1,), (0,)), ((), ())), preferred_element_type=F32,
-                )
-                for dt in range(2)
             ]
             slots = lax.div(lane_of((96, 128)), 32)
             even = roll(early[:, :128] + late[:, 128:], 32)
@@ -446,12 +478,24 @@
             odd = odd + late[:, :128] + now[:, 128:]
             return across(jnp.concatenate([even, odd], axis=1))
 
+        for f in range(7, 1, -1):
+            part_ref[f] = frame_product(core, f)
+        mine_edges = {base: edge_products(core, base, at) for base, at in ((TOP, 0), (BOT, 6))}
+        rows_before(3)
+        later_copy(layer, far).wait_recv()
+        normal_before(layer, far)
+        for f in (1, 0):
+            part_ref[f] = frame_product(core, f)
+        from_sibling(0)
         upper = edge_rows(TOP, 0, 0)
         lower = edge_rows(BOT, 6, 2)
         bias = column(bias_col[...], layer)
         keep = jnp.where(layer == 1, 1.0, 0.0)
-        for f in range(8):
-            total = product(0, 9, lambda dt: slice(256 * (f + dt), 256 * (f + dt) + 256))
+
+        def frame(f):
+            if f == 1:
+                from_sibling(1)
+            total = part_ref[f] + frame_product(1 - core, f)
             above = roll(across(total[0:96]), 32)
             below = roll(across(total[192:288]), -32)
             slot = f // 2
@@ -462,65 +506,59 @@
             above = jnp.where(row256 == 0, jnp.concatenate([from_upper, zero], axis=1), above)
             below = jnp.where(row256 == 7, jnp.concatenate([zero, from_lower], axis=1), below)
             result = above + across(total[96:192]) + below + bias
-            here = slice(256 * f, 256 * f + 256)
-            result = result + keep * raw[0, z, :, here].astype(F32)
-            result = result.astype(BF)
-            own[:, here] = result
-
-            @pl.when(layer + 1 < LAYERS)
+            return result + keep * raw[0, z, :, 256 * f:256 * f + 256].astype(F32)
+
+        publish(layer + 1, frame)
+        return carry
+
+    lax.fori_loop(0, LAYERS, layer_step, 0)
+
+    for part in range(4):
+        send_frames(part)
+
+    def send_rows(k, c):
+        part = lax.rem(x + k, 4)
+
+        @pl.when(k > 0)
+        def _():
+            pltpu.make_async_copy(mid.at[part], mid.at[part], mid_recv.at[part]).wait()
+
+        rows = final_t.at[pl.ds(chans, 32)]
+        for i in range(4):
+            to_tile = part * 4 + i
+
+            @pl.when(to_tile == tile)
             def _():
-                raw[layer + 1, z, :, here] = result
-
-        return carry
-
-    lax.fori_loop(0, LAYERS, layer_step, 0)
-
-    for part in range(4):
-        for block in range(2):
-            at = 512 * part + 128 * block
-            one = own[:, at:at + 128].astype(F32)
-            two = own[:, at + 256:at + 384].astype(F32)
-            slots_out[part * 4 + 2 * block] = jnp.where(lane128 < 64, one, roll(two, 64)).astype(BF)
-            slots_out[part * 4 + 2 * block + 1] = jnp.where(lane128 < 64, roll(one, 64), two).astype(BF)
-
-    def send_out(slot, c):
-        to_tm = y * 4 + lax.div(slot, 4)
-        to_tile = x * 4 + lax.rem(slot, 4)
-        to_self = jnp.logical_and(to_tm == tm, to_tile == tile)
-        rows = final_t.at[pl.ds(chans, 32)]
-
-        @pl.when(to_self)
-        def _():
-            pltpu.make_async_copy(slots_out.at[slot], rows, fin_recv).start()
-
-        @pl.when(jnp.logical_not(to_self))
-        def _():
-            remote(slots_out.at[slot], rows, fin_send, fin_recv, to_tm, to_tile).start()
+                pltpu.make_async_copy(mid.at[part, i], rows, fin_recv).start()
+
+            @pl.when(to_tile != tile)
+            def _():
+                remote(mid.at[part, i], rows, fin_send, fin_recv, tm, to_tile).start()
 
         return c
 
-    lax.fori_loop(0, 16, send_out, 0)
+    lax.fori_loop(0, 4, send_rows, 0)
     pltpu.make_async_copy(final_t, final_t, fin_recv).wait()
     out_ref[...] = final_t[...].astype(F32).T.astype(BF).reshape(2, 2, 32, 512)
 
 
-    def sent(ref, sem):
-        @pl.when(own_x)
-        def _():
-            pltpu.make_async_copy(ref.at[0:15], ref.at[0:15], sem).wait()
-
-        @pl.when(jnp.logical_not(own_x))
-        def _():
-            pltpu.make_async_copy(ref, ref, sem).wait()
-
-    sent(slots_in, a2a_send)
-    sent(slots_out, fin_send)
+    @pl.when(own_x)
+    def _():
+        pltpu.make_async_copy(slots_in.at[0:15], slots_in.at[0:15], a2a_send).wait()
+
+    @pl.when(jnp.logical_not(own_x))
+    def _():
+        pltpu.make_async_copy(slots_in, slots_in, a2a_send).wait()
+
+    pltpu.make_async_copy(slots_in.at[0:15], slots_in.at[0:15], fin_send).wait()
+    pltpu.make_async_copy(mid.at[0:3], mid.at[0:3], mid_send).wait()
 
     def drain(layer, c):
         for copy in halo_copies(layer):
             copy.wait_send()
         pltpu.make_async_copy(stat_in.at[layer], stat_in.at[layer], stat_send.at[layer]).wait()
-        pltpu.make_async_copy(coef.at[layer, 0:7], coef.at[layer, 0:7], coef_send.at[layer]).wait()
+        for k in range(1, 8):
+            coef_copy(layer, k).wait_send()
         for entry in ring_order:
             ring_copy(layer, *entry).wait_send()
 
@@ -552,28 +590,31 @@
             pltpu.VMEM((3, 27, 32, 512), BF),
             pltpu.VMEM((512, 128), BF),
             pltpu.VMEM((16, 32, 128), BF),
-            pltpu.VMEM((3, 8, 32, SENT), BF),
+            pltpu.VMEM((4, 8, 32, SENT), BF),
             pltpu.VMEM((3, 8, 32, 512), BF),
-            pltpu.VMEM((32, 2048), BF),
+            pltpu.VMEM((4, 32, 256), BF),
+            pltpu.VMEM((4, 32, 256), BF),
             pltpu.VMEM((3, 32, 256), BF),
             pltpu.VMEM((3, 32, 256), BF),
             pltpu.VMEM((3, 32, 256), BF),
             pltpu.VMEM((3, 32, 256), BF),
-            pltpu.VMEM((3, 32, 256), BF),
-            pltpu.VMEM((3, 32, 256), BF),
-            pltpu.VMEM((3, 8, 128), F32),
+            pltpu.VMEM((4, 8, 128), F32),
             pltpu.VMEM((3, 15, 8, 128), F32),
             pltpu.VMEM((4, 128, 128), F32),
             pltpu.VMEM((3, 8, 8, 128), F32),
             pltpu.VMEM((3, 8, 2, 32, LANES), BF),
-            pltpu.VMEM((16, 32, 128), BF),
+            pltpu.VMEM((4, 4, 32, 128), BF),
+            pltpu.VMEM((4, 4, 32, 128), BF),
             pltpu.VMEM((512, 128), BF),
             pltpu.VMEM((8, 512), F32),
             pltpu.VMEM((8, 2, 32, 128), F32),
             pltpu.VMEM((32, 128), F32),
-            dma((4,)), dma, dma, dma, dma, dma, dma((3,)), dma((3,)), dma((3,)), dma((3,)),
+            pltpu.VMEM((6, 8, 32, 128), F32),
+            pltpu.VMEM((2, 3, 27, 32, 256), BF),
+            pltpu.VMEM((8, 288, 256), F32),
+            dma((4,)), dma, dma, dma, dma, dma((4,)), dma, dma, dma((3,)), dma((3,)), dma((3, 8)), dma((3, 8)),
             dma((3, 4)), dma((3, 4)), dma((3, 8)), dma((3, 8)),
-            dma((3, 24)), dma((3, 24)), dma((3, 2, 8)), dma((3, 2, 8)),
+            dma((3, 24)), dma((3, 24)), dma((3, 2, 8)), dma((3, 2)),
         ],
         compiler_params=pltpu.CompilerParams(
             collective_id=0, has_side_effects=True, vmem_limit_bytes=64 * 1024 * 1024

time: 122 us -> 107 us (0.88)
  Pallas kernels: 119 us -> 106 us
    pallas_call x1, Pallas kernels: 119 us -> 106 us  [on_device(): pl.pallas_call(kernel, out_shape=jax.ShapeDtypeStruct((2, 2, 32, 512), BF...]
where the time goes in v4:
time: 107 us
  Pallas kernels  106 us (99%)
  local copies, waits for them, and re-layouts  1.57 us (1%)
    pallas_call x1, Pallas kernels, on_device(): pl.pallas_call(kernel, out_shape=jax.ShapeDtypeStruct((2, 2, 32, 512), BF...  106 us

profile of v4, /device:TPU:3, one launch (start us, length us, event | category | flops | bytes accessed | tf_op | source)
XLA Modules:
  0.0 107.1 jit_solution(6555360697136444456)
XLA Ops:
  0.0 105.5 %shard_map.55 = bf16[2,2,32,512]{3,2,1,0:T(8,128)(2,1)} custom-call(bf16[2,2,32,512]{3,2,1,0:T(8,128)(2,1)} %lat_hbm.1, f32[3,512]{1,0:T(4,128)} %gain_hbm.1, f32[3,512]{1,0:T(4,128)} %shift_hbm.1, bf16[3,27,32,512]{3,2,1,0:T(8,128)(2,1)} %w_hbm.1, f32[3,32]{1,0:T(4,128)} %bias_hbm.1), custom_call_target="tpu_custom_call" | custom-call | flops 8000000000 | bytes 3000000 | tf_op jit(solution)/shard_map/pallas_call | solution.py:580
  105.6 1.6 %copy.7 = bf16[2,2,32,512]{3,2,1,0:T(8,128)(2,1)} copy(bf16[2,2,32,512]{3,2,1,0:T(8,128)(2,1)} %shard_map.55) | data formatting | bytes 262144

commit v5 on v4

--- a/solution.py
+++ b/solution.py
@@ -14,8 +14,9 @@
 BOT = MAIN + 256
 PREV = MAIN + 512
 LANES = MAIN + 640
-SENT = LANES - 512
-PARTS = ((0, 1024), (1024, 2048), (2048, SENT))
+PARTS = ((0, 512), (512, 1024), (1024, 1536), (1536, 2048))
+NPARTS = len(PARTS)
+KINDS = ((512, MAIN), (0, 512), (MAIN, LANES))
 PER_FRAME = 32 * 32 * 16
 
 
@@ -37,7 +38,7 @@
 def kernel(
     lat_hbm, gain_hbm, shift_hbm, w_hbm, bias_hbm, out_ref,
     lat_ref, gain_ref, shift_ref, bias_ref,
-    w_ref, local_t, slots_in, raw, before, top_out, bot_out, top_in, bot_in, top_prev, bot_prev,
+    w_ref, local_t, slots_in, raw, before, top_out, bot_out, top_in, bot_in, last_out, left_prev, right_prev,
     stat_out, stat_in, mask_ref, coef, y_ref, slots_out, mid, final_t, par_ref, column_ref, bias_col, table_ref, wk_ref, part_ref,
     in_sem, w_sem, a2a_send, a2a_recv, mid_send, mid_recv, fin_send, fin_recv, stat_send, stat_recv, coef_send, coef_recv,
     halo_send, halo_recv, later_send, later_recv, ring_send, ring_recv, sib_send, sib_recv,
@@ -175,8 +176,6 @@
 
     def publish(index, frames):
         sums = jnp.zeros((32, 128), F32)
-        tops = [jnp.zeros((32, 128), F32)] * 2
-        bots = [jnp.zeros((32, 128), F32)] * 2
         for f in range(7, -1, -1):
             values = frames(f).astype(BF)
             raw[index, z, :, 256 * f:256 * f + 256] = values
@@ -185,12 +184,6 @@
             second = jnp.sum(values * values, axis=1, keepdims=True)
             sums = jnp.where(lane128 == f, first, sums)
             sums = jnp.where(lane128 == 8 + f, second, sums)
-            slot = f // 2
-            tops[f % 2] = jnp.where(slot128 == slot, roll(values[:, :128], 32 * slot), tops[f % 2])
-            bots[f % 2] = jnp.where(slot128 == slot, roll(values[:, 128:], 32 * slot - 96), bots[f % 2])
-        for i in range(2):
-            top_out[index, :, 128 * i:128 * i + 128] = tops[i].astype(BF)
-            bot_out[index, :, 128 * i:128 * i + 128] = bots[i].astype(BF)
         low = jnp.sum(sums[0:16], axis=0, keepdims=True)
         high = jnp.sum(sums[16:32], axis=0, keepdims=True)
         sub8 = lax.broadcasted_iota(jnp.int32, (8, 128), 0)
@@ -229,15 +222,15 @@
     def ring_copy(layer, way, step, part):
         owner = lax.rem(z + 8 + ((1 - step) if way == 0 else (step - 1)), 8)
         piece = raw.at[layer, owner, :, slice(*PARTS[part])]
-        at = (way * 4 + step - 1) * 3 + part
+        at = (way * 4 + step - 1) * NPARTS + part
         return remote(
             piece, piece, ring_send.at[layer, at], ring_recv.at[layer, at], tm, right if way == 0 else left
         )
 
     ring_order = [
         (way, step, part)
-        for step in range(1, 5) for part in range(3) for way in (0, 1)
-        if step < 4 or (part == 1) == (way == 1)
+        for step in range(1, 5) for part in range(NPARTS) for way in (0, 1)
+        if step < 4 or (2 * part >= NPARTS) == (way == 1)
     ]
 
     def later_copy(layer, owner):
@@ -247,7 +240,7 @@
         )
 
     def sib_copy(layer, owner, kind):
-        piece = y_ref.at[layer, owner, core, :, slice(*((512, LANES), (0, 512))[kind])]
+        piece = y_ref.at[layer, owner, core, :, slice(*KINDS[kind])]
         return remote(
             piece, piece, sib_send.at[layer, kind, owner], sib_recv.at[layer, kind], tm, sibling
         )
@@ -258,18 +251,20 @@
             coef.at[layer, z], coef.at[layer, z], coef_send.at[layer, k], coef_recv.at[layer, k], tm, to
         )
 
-    def halo_copies(layer):
+    def halo_copies(layer, owner):
         to_left, to_right = lax.rem(x + 3, 4), lax.rem(x + 1, 4)
         later = lax.rem(y + 1, 4)
         plan = [
             (top_out, bot_in, y * 4 + to_left), (bot_out, top_in, y * 4 + to_right),
-            (top_out, bot_prev, later * 4 + to_left), (bot_out, top_prev, later * 4 + to_right),
+            (last_out, right_prev, later * 4 + to_left), (last_out, left_prev, later * 4 + to_right),
         ]
-        copies = [
-            remote(src.at[layer], dst.at[layer], halo_send.at[layer, i], halo_recv.at[layer, i], to, tile)
+        return [
+            remote(
+                src.at[layer, owner], dst.at[layer, owner], halo_send.at[layer, i, owner],
+                halo_recv.at[layer, i, owner], to, tile,
+            )
             for i, (src, dst, to) in enumerate(plan)
-        ]
-        return copies
+        ] + [later_copy(layer, owner)]
 
     def stat_copy(layer, k):
         other = lax.rem(tm + k, 16)
@@ -294,25 +289,31 @@
             values = raw[layer, owner, :, 256 * f:256 * f + 256].astype(F32)
             values = (values - average[:, j:j + 1]) * scaled[:, 16 + j:17 + j] + wide
             y_ref[layer, owner, core, :, 256 * j:256 * j + 256] = silu(values).astype(BF)
-        for b in range(5):
-            if b == 4:
-                frames = (0, 1, 0, 1)
-                outside = (slot128 < 2) & (x == 0) | (slot128 >= 2) & (x == 3)
-            else:
-                frames = [b % 2 + 2 + 2 * s for s in range(4)]
-                outside = (x == 0) if b < 2 else (x == 3)
-            at = 2048 + 128 * b
-            values = raw[layer, owner, :, at:at + 128].astype(F32)
-            average_at, scaled_at = average[:, frames[0]:frames[0] + 1], scaled[:, 16 + frames[0]:17 + frames[0]]
-            for s in range(1, 4):
-                j = frames[s]
-                average_at = jnp.where(slot128 == s, average[:, j:j + 1], average_at)
-                scaled_at = jnp.where(slot128 == s, scaled[:, 16 + j:17 + j], scaled_at)
-            values = jnp.where(outside, 0.0, silu((values - average_at) * scaled_at + shift))
-            y_ref[layer, owner, core, :, MAIN + 128 * b:MAIN + 128 * b + 128] = values.astype(BF)
         sib_copy(layer, owner, 0).start()
 
-    def normal_before(layer, owner):
+    def edges_out(layer, owner):
+        tops = [jnp.zeros((32, 128), F32)] * 2
+        bots = [jnp.zeros((32, 128), F32)] * 2
+        last = jnp.zeros((32, 128), F32)
+        for f in range(8):
+            upper = raw[layer, owner, :, 256 * f:256 * f + 128].astype(F32)
+            lower = raw[layer, owner, :, 256 * f + 128:256 * f + 256].astype(F32)
+            slot = f // 2
+            tops[f % 2] = jnp.where(slot128 == slot, roll(upper, 32 * slot), tops[f % 2])
+            bots[f % 2] = jnp.where(slot128 == slot, roll(lower, 32 * slot - 96), bots[f % 2])
+            if f >= 6:
+                last = jnp.where(slot128 == f - 6, roll(upper, 32 * (f - 6)), last)
+                last = jnp.where(slot128 == f - 4, roll(lower, 32 * (f - 4) - 96), last)
+        for i in range(2):
+            top_out[layer, owner, :, 128 * i:128 * i + 128] = tops[i].astype(BF)
+            bot_out[layer, owner, :, 128 * i:128 * i + 128] = bots[i].astype(BF)
+        last_out[layer, owner] = last.astype(BF)
+        for copy in halo_copies(layer, owner):
+            copy.start()
+
+    def normal_late(layer, owner):
+        for copy in halo_copies(layer, owner):
+            copy.wait_recv()
         average, scaled, shift = coefficients(layer, owner)
         wide = jnp.concatenate([shift, shift], axis=1)
         for j in range(2):
@@ -321,12 +322,35 @@
             values = (values - average[:, j:j + 1]) * scaled[:, 16 + j:17 + j] + wide
             y_ref[layer, owner, core, :, 256 * j:256 * j + 256] = silu(values).astype(BF)
         sib_copy(layer, owner, 1).start()
+        for b in range(5):
+            if b == 4:
+                frames = (0, 1, 0, 1)
+                outside = (slot128 < 2) & (x == 0) | (slot128 >= 2) & (x == 3)
+                first = top_in[layer, owner, :, 0:128].astype(F32)
+                second = bot_in[layer, owner, :, 0:128].astype(F32)
+                starts = jnp.where(slot128 == 0, first, roll(first, 32))
+                starts = jnp.where(slot128 < 2, starts, jnp.where(slot128 == 2, roll(second, 64), roll(second, 96)))
+                values = jnp.where(
+                    slot128 < 2, roll(left_prev[layer, owner].astype(F32), 64),
+                    roll(right_prev[layer, owner].astype(F32), 64),
+                )
+                values = jnp.where(opening, starts, values)
+            else:
+                frames = [b % 2 + 2 + 2 * s for s in range(4)]
+                outside = (x == 0) if b < 2 else (x == 3)
+                rows = top_in if b < 2 else bot_in
+                values = rows[layer, owner, :, 128 * (b % 2):128 * (b % 2) + 128].astype(F32)
+            average_at, scaled_at = average[:, frames[0]:frames[0] + 1], scaled[:, 16 + frames[0]:17 + frames[0]]
+            for s in range(1, 4):
+                j = frames[s]
+                average_at = jnp.where(slot128 == s, average[:, j:j + 1], average_at)
+                scaled_at = jnp.where(slot128 == s, scaled[:, 16 + j:17 + j], scaled_at)
+            values = jnp.where(outside, 0.0, silu((values - average_at) * scaled_at + shift))
+            y_ref[layer, owner, core, :, MAIN + 128 * b:MAIN + 128 * b + 128] = values.astype(BF)
+        sib_copy(layer, owner, 2).start()
 
     def layer_step(layer, carry):
-        halos = halo_copies(layer)
-        for copy in halos:
-            copy.start()
-        for part in range(2):
+        for part in range(NPARTS):
             for way in (0, 1):
                 ring_copy(layer, way, 1, part).start()
 
@@ -335,7 +359,7 @@
             return c
 
         lax.fori_loop(1, 16, send_stat, 0)
-        later_copy(layer, z).start()
+        edges_out(layer, z)
 
         @pl.when(layer == 0)
         def _():
@@ -343,21 +367,15 @@
 
         lax.fori_loop(27 * layer, 27 * layer + 27, split_w, 0)
 
-        for copy in halos:
-            copy.wait_recv()
-        raw[layer, z, :, 2048:2304] = top_in[layer]
-        raw[layer, z, :, 2304:2560] = bot_in[layer]
-        values = jnp.zeros((32, 128), F32)
-        for i, (now, earlier) in enumerate(((top_in, top_prev), (bot_in, bot_prev))):
-            first = now[layer, :, 0:128].astype(F32)
-            for b in range(2):
-                last = earlier[layer, :, 128 * b:128 * b + 128].astype(F32)
-                slot = 2 * i + b
-                moved = jnp.where(opening, roll(first, 32 * slot), roll(last, 32 * slot - 96))
-                values = jnp.where(slot128 == slot, moved, values)
-        raw[layer, z, :, 2560:2688] = values.astype(BF)
-        for way in (0, 1):
-            ring_copy(layer, way, 1, 2).start()
+        def both(work):
+            def one(way, c):
+                work(way)
+                return c
+
+            lax.fori_loop(0, 2, one, 0)
+
+        def at_distance(step):
+            return lambda way: lax.rem(z + 8 + (1 - 2 * way) * step, 8)
 
         def pass_on(at_step):
             for way, step, part in ring_order:
@@ -365,9 +383,11 @@
                     ring_copy(layer, way, step, part).wait_recv()
                     if (way, step + 1, part) in ring_order:
                         ring_copy(layer, way, step + 1, part).start()
-            for way in (0, 1) if at_step < 4 else (1,):
-                owner = lax.rem(z + 8 + (-at_step if way == 0 else at_step), 8)
-                later_copy(layer, owner).start()
+            owner = at_distance(at_step)
+            if at_step < 4:
+                both(lambda way: edges_out(layer, owner(way)))
+            else:
+                edges_out(layer, owner(0))
 
         pass_on(1)
 
@@ -395,46 +415,30 @@
         normal_own(layer, z)
         pass_on(2)
 
-        def both(work):
-            def one(way, c):
-                work(way)
-                return c
-
-            lax.fori_loop(0, 2, one, 0)
-
-        def at_distance(step):
-            return lambda way: lax.rem(z + 8 + (1 - 2 * way) * step, 8)
-
         def own_rows(step):
             owner = at_distance(step)
             coef_copy(layer, step).wait_recv()
             coef_copy(layer, 8 - step).wait_recv()
             both(lambda way: normal_own(layer, owner(way)))
 
-        def rows_before(step):
+        def late_rows(step):
             owner = at_distance(step)
-
-            def work(way):
-                later_copy(layer, owner(way)).wait_recv()
-                normal_before(layer, owner(way))
-
-            both(work)
+            both(lambda way: normal_late(layer, owner(way)))
 
         pass_on(3)
         own_rows(1)
         own_rows(2)
         own_rows(3)
-        later_copy(layer, z).wait_recv()
-        normal_before(layer, z)
-        rows_before(1)
-        rows_before(2)
+        normal_late(layer, z)
+        late_rows(1)
+        late_rows(2)
         pass_on(4)
         far = lax.rem(z + 4, 8)
         coef_copy(layer, 4).wait_recv()
         normal_own(layer, far)
 
         def from_sibling(kind):
-            piece = y_ref.at[layer, :, 1 - core, :, slice(*((512, LANES), (0, 512))[kind])]
+            piece = y_ref.at[layer, :, 1 - core, :, slice(*KINDS[kind])]
             pltpu.make_async_copy(piece, piece, sib_recv.at[layer, kind]).wait()
 
         def product(half, first_offset, count, steps, lanes_at, width):
@@ -480,22 +484,25 @@
 
         for f in range(7, 1, -1):
             part_ref[f] = frame_product(core, f)
-        mine_edges = {base: edge_products(core, base, at) for base, at in ((TOP, 0), (BOT, 6))}
-        rows_before(3)
-        later_copy(layer, far).wait_recv()
-        normal_before(layer, far)
+        late_rows(3)
+        normal_late(layer, far)
         for f in (1, 0):
             part_ref[f] = frame_product(core, f)
+        mine_edges = {base: edge_products(core, base, at) for base, at in ((TOP, 0), (BOT, 6))}
         from_sibling(0)
+        for f in range(7, 1, -1):
+            part_ref[f] = part_ref[f] + frame_product(1 - core, f)
+        from_sibling(1)
+        from_sibling(2)
         upper = edge_rows(TOP, 0, 0)
         lower = edge_rows(BOT, 6, 2)
         bias = column(bias_col[...], layer)
         keep = jnp.where(layer == 1, 1.0, 0.0)
 
         def frame(f):
-            if f == 1:
-                from_sibling(1)
-            total = part_ref[f] + frame_product(1 - core, f)
+            total = part_ref[f]
+            if f < 2:
+                total = total + frame_product(1 - core, f)
             above = roll(across(total[0:96]), 32)
             below = roll(across(total[192:288]), -32)
             slot = f // 2
@@ -554,8 +561,6 @@
     pltpu.make_async_copy(mid.at[0:3], mid.at[0:3], mid_send).wait()
 
     def drain(layer, c):
-        for copy in halo_copies(layer):
-            copy.wait_send()
         pltpu.make_async_copy(stat_in.at[layer], stat_in.at[layer], stat_send.at[layer]).wait()
         for k in range(1, 8):
             coef_copy(layer, k).wait_send()
@@ -563,8 +568,9 @@
             ring_copy(layer, *entry).wait_send()
 
         def drain_owner(owner, carry):
-            later_copy(layer, owner).wait_send()
-            for kind in range(2):
+            for copy in halo_copies(layer, owner):
+                copy.wait_send()
+            for kind in range(3):
                 sib_copy(layer, owner, kind).wait_send()
             return carry
 
@@ -590,14 +596,15 @@
             pltpu.VMEM((3, 27, 32, 512), BF),
             pltpu.VMEM((512, 128), BF),
             pltpu.VMEM((16, 32, 128), BF),
-            pltpu.VMEM((4, 8, 32, SENT), BF),
+            pltpu.VMEM((4, 8, 32, 2048), BF),
             pltpu.VMEM((3, 8, 32, 512), BF),
-            pltpu.VMEM((4, 32, 256), BF),
-            pltpu.VMEM((4, 32, 256), BF),
-            pltpu.VMEM((3, 32, 256), BF),
-            pltpu.VMEM((3, 32, 256), BF),
-            pltpu.VMEM((3, 32, 256), BF),
-            pltpu.VMEM((3, 32, 256), BF),
+            pltpu.VMEM((3, 8, 32, 256), BF),
+            pltpu.VMEM((3, 8, 32, 256), BF),
+            pltpu.VMEM((3, 8, 32, 256), BF),
+            pltpu.VMEM((3, 8, 32, 256), BF),
+            pltpu.VMEM((3, 8, 32, 128), BF),
+            pltpu.VMEM((3, 8, 32, 128), BF),
+            pltpu.VMEM((3, 8, 32, 128), BF),
             pltpu.VMEM((4, 8, 128), F32),
             pltpu.VMEM((3, 15, 8, 128), F32),
             pltpu.VMEM((4, 128, 128), F32),
@@ -613,8 +620,8 @@
             pltpu.VMEM((2, 3, 27, 32, 256), BF),
             pltpu.VMEM((8, 288, 256), F32),
             dma((4,)), dma, dma, dma, dma, dma((4,)), dma, dma, dma((3,)), dma((3,)), dma((3, 8)), dma((3, 8)),
-            dma((3, 4)), dma((3, 4)), dma((3, 8)), dma((3, 8)),
-            dma((3, 24)), dma((3, 24)), dma((3, 2, 8)), dma((3, 2)),
+            dma((3, 4, 8)), dma((3, 4, 8)), dma((3, 8)), dma((3, 8)),
+            dma((3, 8 * NPARTS)), dma((3, 8 * NPARTS)), dma((3, 3, 8)), dma((3, 3)),
         ],
         compiler_params=pltpu.CompilerParams(
             collective_id=0, has_side_effects=True, vmem_limit_bytes=64 * 1024 * 1024

time: 107 us -> 105 us (0.981)
  Pallas kernels: 106 us -> 103 us
    pallas_call x1, Pallas kernels: 106 us -> 103 us  [on_device(): pl.pallas_call(kernel, out_shape=jax.ShapeDtypeStruct((2, 2, 32, 512), BF...]
where the time goes in v5:
time: 105 us
  Pallas kernels  103 us (98%)
  local copies, waits for them, and re-layouts  1.57 us (1%)
    pallas_call x1, Pallas kernels, on_device(): pl.pallas_call(kernel, out_shape=jax.ShapeDtypeStruct((2, 2, 32, 512), BF...  103 us

profile of v5, /device:TPU:3, one launch (start us, length us, event | category | flops | bytes accessed | tf_op | source)
XLA Modules:
  0.0 104.8 jit_solution(10683721429005410251)
XLA Ops:
  0.0 103.2 %shard_map.55 = bf16[2,2,32,512]{3,2,1,0:T(8,128)(2,1)} custom-call(bf16[2,2,32,512]{3,2,1,0:T(8,128)(2,1)} %lat_hbm.1, f32[3,512]{1,0:T(4,128)} %gain_hbm.1, f32[3,512]{1,0:T(4,128)} %shift_hbm.1, bf16[3,27,32,512]{3,2,1,0:T(8,128)(2,1)} %w_hbm.1, f32[3,32]{1,0:T(4,128)} %bias_hbm.1), custom_call_target="tpu_custom_call" | custom-call | flops 8000000000 | bytes 3000000 | tf_op jit(solution)/shard_map/pallas_call | solution.py:586
  103.2 1.6 %copy.7 = bf16[2,2,32,512]{3,2,1,0:T(8,128)(2,1)} copy(bf16[2,2,32,512]{3,2,1,0:T(8,128)(2,1)} %shard_map.55) | data formatting | bytes 262144

commit v6 on v5

--- a/solution.py
+++ b/solution.py
@@ -39,7 +39,7 @@
     lat_hbm, gain_hbm, shift_hbm, w_hbm, bias_hbm, out_ref,
     lat_ref, gain_ref, shift_ref, bias_ref,
     w_ref, local_t, slots_in, raw, before, top_out, bot_out, top_in, bot_in, last_out, left_prev, right_prev,
-    stat_out, stat_in, mask_ref, coef, y_ref, slots_out, mid, final_t, par_ref, column_ref, bias_col, table_ref, wk_ref, part_ref,
+    stat_out, stat_in, mask_ref, coef, y_ref, slots_out, mid, final_t, par_ref, column_ref, bias_col, table_ref, wk_ref, part_ref, done_ref,
     in_sem, w_sem, a2a_send, a2a_recv, mid_send, mid_recv, fin_send, fin_recv, stat_send, stat_recv, coef_send, coef_recv,
     halo_send, halo_recv, later_send, later_recv, ring_send, ring_recv, sib_send, sib_recv,
 ):
@@ -391,6 +391,8 @@
 
         pass_on(1)
 
+        pass_on(2)
+
         pltpu.make_async_copy(stat_in.at[layer], stat_in.at[layer], stat_recv.at[layer]).wait()
         sources = [jnp.zeros((8, 128), F32)] * 4
         for s in range(16):
@@ -413,7 +415,6 @@
         for k in (1, 7, 2, 6, 3, 5, 4):
             coef_copy(layer, k).start()
         normal_own(layer, z)
-        pass_on(2)
 
         def own_rows(step):
             owner = at_distance(step)
@@ -463,8 +464,11 @@
             )
 
         def across(total):
-            before = jnp.where(col256 >= 1, roll(total[0:32], 1), 0.0)
-            after = jnp.where(col256 <= 30, roll(total[64:96], -1), 0.0)
+            lanes = [slice(at, at + 128) for at in range(0, total.shape[1], 128)]
+            before = jnp.concatenate([roll(total[0:32, at], 1) for at in lanes], axis=1)
+            after = jnp.concatenate([roll(total[64:96, at], -1) for at in lanes], axis=1)
+            before = jnp.where(col256 >= 1, before, 0.0)
+            after = jnp.where(col256 <= 30, after, 0.0)
             return before + total[32:64] + after
 
         def edge_rows(base, first_offset, slot):
@@ -482,6 +486,11 @@
             odd = odd + late[:, :128] + now[:, 128:]
             return across(jnp.concatenate([even, odd], axis=1))
 
+        def combine(total):
+            above = jnp.where(row256 == 0, 0.0, roll(across(total[0:96]), 32))
+            below = jnp.where(row256 == 7, 0.0, roll(across(total[192:288]), -32))
+            return above + across(total[96:192]) + below
+
         for f in range(7, 1, -1):
             part_ref[f] = frame_product(core, f)
         late_rows(3)
@@ -491,7 +500,7 @@
         mine_edges = {base: edge_products(core, base, at) for base, at in ((TOP, 0), (BOT, 6))}
         from_sibling(0)
         for f in range(7, 1, -1):
-            part_ref[f] = part_ref[f] + frame_product(1 - core, f)
+            done_ref[f] = combine(part_ref[f] + frame_product(1 - core, f))
         from_sibling(1)
         from_sibling(2)
         upper = edge_rows(TOP, 0, 0)
@@ -500,19 +509,15 @@
         keep = jnp.where(layer == 1, 1.0, 0.0)
 
         def frame(f):
-            total = part_ref[f]
-            if f < 2:
-                total = total + frame_product(1 - core, f)
-            above = roll(across(total[0:96]), 32)
-            below = roll(across(total[192:288]), -32)
+            body = done_ref[f] if f >= 2 else combine(part_ref[f] + frame_product(1 - core, f))
             slot = f // 2
             edge = 128 * (f % 2)
             from_upper = roll(upper[:, edge:edge + 128], -32 * slot)
             from_lower = roll(lower[:, edge:edge + 128], 96 - 32 * slot)
-            zero = jnp.zeros((32, 128), F32)
-            above = jnp.where(row256 == 0, jnp.concatenate([from_upper, zero], axis=1), above)
-            below = jnp.where(row256 == 7, jnp.concatenate([zero, from_lower], axis=1), below)
-            result = above + across(total[96:192]) + below + bias
+            edges = jnp.concatenate(
+                [jnp.where(slot128 == 0, from_upper, 0.0), jnp.where(slot128 == 3, from_lower, 0.0)], axis=1
+            )
+            result = body + edges + bias
             return result + keep * raw[0, z, :, 256 * f:256 * f + 256].astype(F32)
 
         publish(layer + 1, frame)
@@ -619,6 +624,7 @@
             pltpu.VMEM((6, 8, 32, 128), F32),
             pltpu.VMEM((2, 3, 27, 32, 256), BF),
             pltpu.VMEM((8, 288, 256), F32),
+            pltpu.VMEM((8, 32, 256), F32),
             dma((4,)), dma, dma, dma, dma, dma((4,)), dma, dma, dma((3,)), dma((3,)), dma((3, 8)), dma((3, 8)),
             dma((3, 4, 8)), dma((3, 4, 8)), dma((3, 8)), dma((3, 8)),
             dma((3, 8 * NPARTS)), dma((3, 8 * NPARTS)), dma((3, 3, 8)), dma((3, 3)),

time: 105 us -> 103 us (0.981)
  Pallas kernels: 103 us -> 101 us
    pallas_call x1, Pallas kernels: 103 us -> 101 us  [on_device(): pl.pallas_call(kernel, out_shape=jax.ShapeDtypeStruct((2, 2, 32, 512), BF...]
where the time goes in v6:
time: 103 us
  Pallas kernels  101 us (98%)
  local copies, waits for them, and re-layouts  1.57 us (2%)
    pallas_call x1, Pallas kernels, on_device(): pl.pallas_call(kernel, out_shape=jax.ShapeDtypeStruct((2, 2, 32, 512), BF...  101 us

profile of v6, /device:TPU:3, one launch (start us, length us, event | category | flops | bytes accessed | tf_op | source)
XLA Modules:
  0.0 103.0 jit_solution(737329876641043912)
XLA Ops:
  0.0 101.4 %shard_map.55 = bf16[2,2,32,512]{3,2,1,0:T(8,128)(2,1)} custom-call(bf16[2,2,32,512]{3,2,1,0:T(8,128)(2,1)} %lat_hbm.1, f32[3,512]{1,0:T(4,128)} %gain_hbm.1, f32[3,512]{1,0:T(4,128)} %shift_hbm.1, bf16[3,27,32,512]{3,2,1,0:T(8,128)(2,1)} %w_hbm.1, f32[3,32]{1,0:T(4,128)} %bias_hbm.1), custom_call_target="tpu_custom_call" | custom-call | flops 8000000000 | bytes 3000000 | tf_op jit(solution)/shard_map/pallas_call | solution.py:591
  101.4 1.6 %copy.7 = bf16[2,2,32,512]{3,2,1,0:T(8,128)(2,1)} copy(bf16[2,2,32,512]{3,2,1,0:T(8,128)(2,1)} %shard_map.55) | data formatting | bytes 262144

commit v7 on v6

--- a/solution.py
+++ b/solution.py
@@ -354,12 +354,13 @@
             for way in (0, 1):
                 ring_copy(layer, way, 1, part).start()
 
+        edges_out(layer, z)
+
         def send_stat(k, c):
             stat_copy(layer, k).start()
             return c
 
         lax.fori_loop(1, 16, send_stat, 0)
-        edges_out(layer, z)
 
         @pl.when(layer == 0)
         def _():

time: 103 us -> 103 us (level)
  no operation moved by 1% of the time
where the time goes in v7:
time: 103 us
  Pallas kernels  101 us (98%)
  local copies, waits for them, and re-layouts  1.57 us (2%)
    pallas_call x1, Pallas kernels, on_device(): pl.pallas_call(kernel, out_shape=jax.ShapeDtypeStruct((2, 2, 32, 512), BF...  101 us

profile of v7, /device:TPU:3, one launch (start us, length us, event | category | flops | bytes accessed | tf_op | source)
XLA Modules:
  0.0 102.9 jit_solution(9483240916543655452)
XLA Ops:
  0.0 101.4 %shard_map.55 = bf16[2,2,32,512]{3,2,1,0:T(8,128)(2,1)} custom-call(bf16[2,2,32,512]{3,2,1,0:T(8,128)(2,1)} %lat_hbm.1, f32[3,512]{1,0:T(4,128)} %gain_hbm.1, f32[3,512]{1,0:T(4,128)} %shift_hbm.1, bf16[3,27,32,512]{3,2,1,0:T(8,128)(2,1)} %w_hbm.1, f32[3,32]{1,0:T(4,128)} %bias_hbm.1), custom_call_target="tpu_custom_call" | custom-call | flops 8000000000 | bytes 3000000 | tf_op jit(solution)/shard_map/pallas_call | solution.py:592
  101.4 1.6 %copy.7 = bf16[2,2,32,512]{3,2,1,0:T(8,128)(2,1)} copy(bf16[2,2,32,512]{3,2,1,0:T(8,128)(2,1)} %shard_map.55) | data formatting | bytes 262144
